TPU v7x, 512 devices: a whole 4x4x16 slice. The times are simulated.
512 devices in a mesh: dp: 32 (over z, core), expert: 16 (over x, y).
Axes of the slice: x: 4, y: 4, z: 16, core: 2. Of those that a mesh axis runs over, the one named last changes fastest.
Arguments:
- tokens: bfloat16 [65536, 2048], P(('dp', 'expert'))
- targets: bfloat16 [65536, 2048], P(('dp', 'expert'))
- routes: int32 [65536, 8], P(('dp', 'expert')), may hold values from 0 to 15, all different within a row; in each aligned block of 128 rows (0 to 127, 128 to 255, ...) at most 64 rows name the same one
- route_logits: float32 [65536, 8], P(('dp', 'expert')), may hold values from -3 to 3
- slot_order: int32 [65536, 8], P(('dp', 'expert')), may hold values from 0 to 7, each once within a row
- seq_ids: int32 [65536], P(('dp', 'expert')), may hold values from 0 to 63, as said below
- w_gate: bfloat16 [16, 2048, 384], P('expert')
- w_up: bfloat16 [16, 2048, 384], P('expert')
- w_down: bfloat16 [2048, 16, 384], P('dp', 'expert')
Outputs:
- mixed: bfloat16 [65536, 2048], P(('dp', 'expert'))
- seq_loss: float32 [64], replicated
- dual_weight: float32 [64], replicated
- grad_down: float32 [2048, 16, 384], P('dp', 'expert')
Inputs may be any that keep to these rules, and one draw needn't show every extreme that they name: `routes`: in each aligned block of 128 rows (the rows of one device) every expert is named by exactly 64 rows; the 8 numbers of a row differ. `slot_order`: each row is a permutation of 0 to 7. `seq_ids`: sequence numbers never fall along the tokens, and every number names one or more tokens.
All inputs are finite; a program needn't handle non-finite values.
Results may differ from a plain program's by a relative error of at most 0.0046.
Values may be sent and summed in bfloat16 or wider, within the bound.
A program may use at most 64 MiB of HBM per device.

v0:
```python
import jax
import jax.numpy as jnp
from jax import lax
from jax.sharding import PartitionSpec as P

NSEQ = 64
BISECT_STEPS = 40


radius_factor = 2.0


def unchanged(single_value):
    return single_value


def dual_search(seq_loss, pair_total, one_total):
    sum_total = one_total(jnp.sum(seq_loss))

    def advance(step_index, bounds):
        lower, upper = bounds
        middle = 0.5 * (lower + upper)
        excess = jnp.maximum(seq_loss - middle, 0.0)
        square_sum, plain_sum = pair_total((jnp.sum(excess * excess), jnp.sum(excess)))
        is_above = NSEQ * square_sum - radius_factor * plain_sum * plain_sum >= 0.0
        return (jnp.where(is_above, lower, middle), jnp.where(is_above, middle, upper))

    lower, upper = lax.fori_loop(0, BISECT_STEPS, advance, (-sum_total, sum_total))
    excess = jnp.maximum(seq_loss - 0.5 * (lower + upper), 0.0)
    return excess / one_total(jnp.sum(excess))


def route_gates(route_logits, slot_order):
    top_k = slot_order.shape[1]
    columns = lax.broadcasted_iota(jnp.int32, (1, 1, top_k), 2)
    picked = jnp.sum(
        jnp.where(slot_order[:, :, None] == columns, route_logits[:, None, :], 0.0), axis=2
    )
    raised = jnp.exp(picked)
    return raised / jnp.sum(raised, axis=1, keepdims=True)


def by_expert(blocks, groups):
    exp_dev = blocks.shape[0] // groups
    tail_shape = blocks.shape[1:]
    split_view = blocks.reshape((groups, exp_dev) + tail_shape)
    moved_view = jnp.swapaxes(split_view, 0, 1)
    return moved_view.reshape((exp_dev, groups * tail_shape[0]) + tail_shape[1:])


def by_source(local_rows, groups):
    exp_dev = local_rows.shape[0]
    capacity = local_rows.shape[1] // groups
    tail_shape = local_rows.shape[2:]
    split_view = local_rows.reshape((exp_dev, groups, capacity) + tail_shape)
    return jnp.swapaxes(split_view, 0, 1).reshape((exp_dev * groups, capacity) + tail_shape)


def local(tokens, targets, routes, route_logits, slot_order, seq_ids, w_gate, w_up, w_down):
    tok_rows, feat_width = tokens.shape
    top_k = routes.shape[1]
    groups = lax.axis_size("expert")
    exp_dev = w_gate.shape[0]
    experts = exp_dev * groups
    slot_count = tok_rows * top_k
    capacity = slot_count // experts
    grad_scale = float(tok_rows * lax.axis_size("dp") * groups // 8)
    flat_route = routes.reshape(slot_count)
    expert_hot = (flat_route[:, None] == lax.broadcasted_iota(jnp.int32, (1, experts), 1)).astype(
        jnp.int32
    )
    slot_rank = jnp.sum((jnp.cumsum(expert_hot, axis=0) - 1) * expert_hot, axis=1)
    slot_index = flat_route * capacity + slot_rank
    inverse = (
        jnp.zeros((slot_count,), jnp.int32).at[slot_index].set(lax.iota(jnp.int32, slot_count))
    )
    source_row = inverse // top_k
    gate_probs = route_gates(route_logits, slot_order)
    send_rows = tokens[source_row].reshape(experts, capacity, feat_width)
    arrived = lax.all_to_all(send_rows, "expert", split_axis=0, concat_axis=0, tiled=True)
    local_rows = by_expert(arrived, groups)
    gate_proj = jnp.einsum("erd,edh->erh", local_rows, w_gate, preferred_element_type=jnp.float32)
    up_proj = jnp.einsum("erd,edh->erh", local_rows, w_up, preferred_element_type=jnp.float32)
    hidden = (jax.nn.silu(gate_proj) * up_proj).astype(jnp.bfloat16)
    expert_out = jnp.einsum(
        "erh,neh->ern",
        hidden,
        lax.all_gather(w_down, "dp", axis=0, tiled=True),
        preferred_element_type=jnp.float32,
    ).astype(jnp.bfloat16)
    returned = lax.all_to_all(
        by_source(expert_out, groups), "expert", split_axis=0, concat_axis=0, tiled=True
    )
    per_slot = returned.reshape(slot_count, feat_width)[slot_index].reshape(
        tok_rows, top_k, feat_width
    )
    combined = jnp.sum(gate_probs[:, :, None] * per_slot.astype(jnp.float32), axis=1)
    error = combined - targets.astype(jnp.float32)
    error_low = error.astype(jnp.bfloat16)
    sent_error = lax.all_to_all(
        error_low[source_row].reshape(experts, capacity, feat_width),
        "expert",
        split_axis=0,
        concat_axis=0,
        tiled=True,
    )
    seq_hot = seq_ids[:, None] == lax.broadcasted_iota(jnp.int32, (1, NSEQ), 1)
    partial_sq = jnp.sum(jnp.where(seq_hot, jnp.sum(error * error, axis=1)[:, None], 0.0), axis=0)
    counts = jnp.sum(seq_hot.astype(jnp.float32), axis=0)
    seq_sq, seq_len = lax.psum((partial_sq, counts), ("dp", "expert"))
    seq_loss = seq_sq / (seq_len * feat_width)
    dual_weight = dual_search(seq_loss, unchanged, unchanged)
    seq_rate = dual_weight / seq_len
    scaled_gates = grad_scale * gate_probs
    token_rate = jnp.sum(jnp.where(seq_hot, seq_rate[None, :], 0.0), axis=1)
    flat_weight = (scaled_gates * token_rate[:, None]).reshape(slot_count)
    slot_weight = lax.all_to_all(
        flat_weight[inverse].reshape(experts, capacity),
        "expert",
        split_axis=0,
        concat_axis=0,
        tiled=True,
    )
    weight_local = by_expert(slot_weight, groups)
    error_local = by_expert(sent_error, groups)
    scaled = (weight_local[:, :, None] * hidden).astype(jnp.bfloat16)
    grad_down = lax.psum_scatter(
        jnp.einsum("ern,erh->neh", error_local, scaled, preferred_element_type=jnp.float32),
        "dp",
        scatter_dimension=0,
        tiled=True,
    )
    return (combined.astype(jnp.bfloat16), seq_loss, dual_weight, grad_down)


def solution(mesh):
    return jax.shard_map(
        local,
        mesh=mesh,
        in_specs=(
            P(("dp", "expert"), None),
            P(("dp", "expert"), None),
            P(("dp", "expert"), None),
            P(("dp", "expert"), None),
            P(("dp", "expert"), None),
            P(("dp", "expert")),
            P("expert", None, None),
            P("expert", None, None),
            P("dp", "expert", None),
        ),
        out_specs=(P(("dp", "expert"), None), P(), P(), P("dp", "expert", None)),
        check_vma=False,
    )
```

profile of v0, /device:TPU:1, one launch (start us, length us, event | category | flops | bytes accessed | tf_op | source)
XLA Modules:
  0.0 799.7 jit_solution(14870960607679553497)
XLA Ops:
  7.2 0.9 copy.36
  8.3 0.7 broadcast_multiply_fusion.1
  9.0 4.5 reduce-window.6
  14.2 4.3 scatter_custom_fusion
  18.6 6.0 gather_fusion
  24.6 7.6 all-to-all-start
  32.3 0.7 all-gather.2.cloned.1.call-update
  33.0 45.5 %all-to-all-done = bf16[16,64,2048]{2,1,0:T(8,128)(2,1)} async-done(((bf16[16,64,2048]{2,1,0:T(8,128)(2,1)}), bf16[16,64,2048]{2,1,0:T(8,128)(2,1)}, u32[]{:S(2)}, u32[]{:S(2)}) %all-to-all-start) | async-done | bytes 4194336 | tf_op jit(solution)/shard_map/all_to_all | solution.py:80
  78.5 4.6 fusion.5
  83.1 4.6 multiply_convert_fusion.1
  87.7 24.0 %all-gather.2.cloned.1.call-done = bf16[2048,1,384]{2,0,1:T(8,128)(2,1)} async-done(((bf16[64,1,384]{2,0,1:T(8,128)(2,1)}), bf16[2048,1,384]{2,0,1:T(8,128)(2,1)}) %all-gather.2.cloned.1.call-update) | async-done | bytes 1572880 | tf_op jit(solution)/shard_map/all_gather | solution.py:88
  111.8 5.8 convolution_convert_fusion
  117.5 6.7 all-to-all-start.1
  124.5 55.6 %all-to-all-done.1 = bf16[16,64,2048]{2,1,0:T(8,128)(2,1)} async-done(((bf16[16,64,2048]{2,1,0:T(8,128)(2,1)}), bf16[16,64,2048]{2,1,0:T(8,128)(2,1)}, u32[]{:S(2)}, u32[]{:S(2)}) %all-to-all-start.1) | async-done | bytes 4194336 | tf_op jit(solution)/shard_map/all_to_all | solution.py:91
  180.1 11.6 %gather_fusion.1 = bf16[1024,2048]{1,0:T(8,128)(2,1)} fusion(bf16[1024,2048]{1,0:T(8,128)(2,1)} %bitcast.10, s32[1024]{0:T(1024)S(1)} %broadcast_clamp_fusion), kind=kCustom, calls=%fused_computation.1 | custom fusion | bytes 8392704 | tf_op jit(solution)/shard_map/gather | solution.py:94
  191.6 6.6 fusion.1
  198.2 1.0 fusion.10
  199.3 106.9 %all-reduce.1 = (f32[64]{0:T(128)S(1)}, f32[64]{0:T(128)S(1)}) all-reduce(f32[64]{0:T(128)S(1)} %get-tuple-element.40, f32[64]{0:T(128)S(1)} %get-tuple-element.39), channel_id=1, replica_groups=mesh['dp'=32,'expert'=16] {'dp','expert'}, use_global_device_ids=true, to_apply=%region_9.10 | all-reduce | flops 128 | bytes 1024 | tf_op jit(solution)/shard_map/psum | solution.py:110
  306.2 0.6 fusion.21
  307.5 170.9 %while.12 = (s32[]{:T(128)}, f32[]{:T(128)}, f32[]{:T(128)}, f32[64]{0:T(128)S(1)}, s32[]{:T(128)}, /*index=5*/f32[]{:T(128)}, f32[]{:T(128)}, f32[]{:T(128)}, f32[]{:T(128)}) while((s32[]{:T(128)}, f32[]{:T(128)}, f32[]{:T(128)}, f32[64]{0:T(128)S(1)}, s32[]{:T(128)}, /*index=5*/f32[]{:T(128)}, f32[]{:T(128)}, f32[]{:T(128)}, ...), condition=%wide.region_16.17_spmd, body=%wide.region_13.16_spmd.sunk | while | flops 329 | bytes 468 | solution.py:28
  308.2 0.6 fusion.27
  312.4 0.6 fusion.27
  316.7 0.6 fusion.27
  321.0 0.6 fusion.27
  325.2 0.6 fusion.27
  329.5 0.6 fusion.27
  333.8 0.6 fusion.27
  338.1 0.6 fusion.27
  342.3 0.6 fusion.27
  346.6 0.6 fusion.27
  350.9 0.6 fusion.27
  355.1 0.6 fusion.27
  359.4 0.6 fusion.27
  363.7 0.6 fusion.27
  368.0 0.6 fusion.27
  372.2 0.6 fusion.27
  376.5 0.6 fusion.27
  380.8 0.6 fusion.27
  385.1 0.6 fusion.27
  389.3 0.6 fusion.27
  393.6 0.6 fusion.27
  402.1 0.6 fusion.27
  406.4 0.6 fusion.27
  410.7 0.6 fusion.27
  415.0 0.6 fusion.27
  419.2 0.6 fusion.27
  423.5 0.6 fusion.27
  427.8 0.6 fusion.27
  432.0 0.6 fusion.27
  436.3 0.6 fusion.27
  440.6 0.6 fusion.27
  479.6 1.2 multiply_divide_fusion
  481.1 4.5 gather_fusion.2
  485.6 0.7 all_to_all.17
  486.3 3.5 all-to-all-start.2
  489.8 6.0 gather_fusion.3
  496.1 6.4 all-to-all-start.3
  503.1 0.7 reduce.3
  503.8 50.5 %all-to-all-done.3 = bf16[16,64,2048]{2,1,0:T(8,128)(2,1)} async-done(((bf16[16,64,2048]{2,1,0:T(8,128)(2,1)}), bf16[16,64,2048]{2,1,0:T(8,128)(2,1)}, u32[]{:S(2)}, u32[]{:S(2)}) %all-to-all-start.3) | async-done | bytes 4194336 | tf_op jit(solution)/shard_map/all_to_all | solution.py:100
  554.3 5.8 convolution_bitcast_fusion
  560.1 8.5 %copy.41 = f32[2048,1,384]{2,1,0:T(1,128)} copy(f32[2048,1,384]{0,2,1:T(8,128)} %convolution_bitcast_fusion) | data formatting | bytes 6291456 | tf_op jit(solution)/shard_map/ern,erh->neh/transpose | solution.py:128
  568.7 1.3 dynamic-slice
  570.6 220.7 %all-reduce.4.cloned.1.call-done = f32[2048,1,384]{2,1,0:T(1,128)} async-done(((f32[2048,1,384]{2,1,0:T(1,128)}), f32[2048,1,384]{2,1,0:T(1,128)}) %all-reduce.4.cloned.1.call-update) | async-done | bytes 3145744
  791.3 1.6 constant_dynamic-slice_fusion
  (58 shorter events, 8.4 us)
Async XLA Ops:
  7.2 71.3 %copy-start = (bf16[1,2048,384]{2,1,0:T(8,128)(2,1)S(1)}, bf16[1,2048,384]{2,1,0:T(8,128)(2,1)}, u32[]{:S(2)}) copy-start(bf16[1,2048,384]{2,1,0:T(8,128)(2,1)} %param.17) | copy-start | bytes 4718596
  7.2 11.4 %copy-start.1 = (bf16[128,2048]{1,0:T(8,128)(2,1)S(1)}, bf16[128,2048]{1,0:T(8,128)(2,1)}, u32[]{:S(2)}) copy-start(bf16[128,2048]{1,0:T(8,128)(2,1)} %param.11) | copy-start | bytes 1572868
  24.6 53.9 %all-to-all-start = ((bf16[16,64,2048]{2,1,0:T(8,128)(2,1)}), bf16[16,64,2048]{2,1,0:T(8,128)(2,1)}, u32[]{:S(2)}, u32[]{:S(2)}) async-start(bf16[16,64,2048]{2,1,0:T(8,128)(2,1)} %bitcast.46), calls=%async_computation | async-start | bytes 8388608 | tf_op jit(solution)/shard_map/all_to_all | solution.py:80
  32.2 79.6 %all-gather.2.cloned.1.call-start = ((), (), s32[]{:S(2)}) async-start(), calls=%async_computation.4 | async-start | bytes 1622016 | tf_op jit(solution)/shard_map/all_gather | solution.py:88
  78.5 4.6 copy-start.7
  117.5 6.7 copy-start.4
  117.5 6.7 copy-start.5
  117.5 62.5 %all-to-all-start.1 = ((bf16[16,64,2048]{2,1,0:T(8,128)(2,1)}), bf16[16,64,2048]{2,1,0:T(8,128)(2,1)}, u32[]{:S(2)}, u32[]{:S(2)}) async-start(bf16[16,64,2048]{2,1,0:T(8,128)(2,1)} %bitcast.47), calls=%async_computation.1 | async-start | bytes 8388608 | tf_op jit(solution)/shard_map/all_to_all | solution.py:91
  191.6 6.6 copy-start.2
  191.6 7.6 copy-start.6
  478.4 17.5 %copy-start.3 = (f32[64]{0:T(128)}, f32[64]{0:T(128)S(1)}, u32[]{:S(2)}) copy-start(f32[64]{0:T(128)S(1)} %get-tuple-element.129) | copy-start | bytes 772
  486.3 9.8 %all-to-all-start.2 = ((f32[16,1,64]{2,1,0:T(1,128)}), f32[16,1,64]{2,1,0:T(1,128)S(1)}, u32[]{:S(2)}, u32[]{:S(2)}) async-start(f32[16,1,64]{2,1,0:T(1,128)} %all_to_all.17), calls=%async_computation.2 | async-start | bytes 16384 | tf_op jit(solution)/shard_map/all_to_all | solution.py:117
  496.1 58.3 %all-to-all-start.3 = ((bf16[16,64,2048]{2,1,0:T(8,128)(2,1)}), bf16[16,64,2048]{2,1,0:T(8,128)(2,1)}, u32[]{:S(2)}, u32[]{:S(2)}) async-start(bf16[16,64,2048]{2,1,0:T(8,128)(2,1)} %bitcast.45), calls=%async_computation.3 | async-start | bytes 8388608 | tf_op jit(solution)/shard_map/all_to_all | solution.py:100
  502.5 288.8 %all-reduce.4.cloned.1.call-start = ((), (), s32[]{:S(2)}) async-start(), calls=%async_computation.5 | async-start | bytes 6291456
Sparse Core Ops, SparseCore 0:
  35.2 76.5 all-gather.1
  568.8 222.4 all-reduce.3
where the time goes:
time: 802 us; the launch traced here: 800 us
  waiting for transfers between devices  397 us (50%)
  loops' own time  147 us (18%)
  blocking collectives  107 us (13%)
  local copies, waits for them, and re-layouts  47 us (6%)
  other arithmetic  40.3 us (5%)
  starting transfers between devices  24.3 us (3%)
  matrix products  20.8 us (3%)
  between operations  16.2 us (2%)
    unnamed x3, waiting for transfers between devices  221 us
    another operation x1, loops' own time, dual_search(): lax.fori_loop(0, BISECT_STEPS, advance, (-sum_total, sum_total))  147 us
    psum x1, blocking collectives, local(): seq_sq, seq_len = lax.psum((partial_sq, counts), ('dp', 'expert'))  107 us
    all_to_all x1, waiting for transfers between devices, local(): lax.all_to_all(by_source(expert_out, groups), 'expert', split_axis=0, con...  55.6 us
    all_to_all x1, waiting for transfers between devices, local(): lax.all_to_all(error_low[source_row].reshape(experts, capacity, feat_widt...  50.5 us
    all_to_all x1, waiting for transfers between devices, local(): lax.all_to_all(send_rows, 'expert', split_axis=0, concat_axis=0, tiled=True)  45.5 us
    reduce_sum x40, other arithmetic, advance(): jnp.sum(excess)  24.1 us
    all_gather x1, waiting for transfers between devices, local(): lax.all_gather(w_down, 'dp', axis=0, tiled=True)  24 us
  transfers between devices with their start and end apart: 6, of which 6 were waited for; matrix products, arithmetic and copies ran while one was open for 2% of the time, Pallas kernels for 0%

commit v1 on v0

v1 whole, which is shorter than its diff:
```python
import functools

import jax
import jax.numpy as jnp
from jax import lax
from jax.experimental import pallas as pl
from jax.experimental.pallas import tpu as pltpu
from jax.sharding import PartitionSpec as P

MESH = pl.DeviceIdType.MESH
SIDE = 4
NSEQ = 64
CAP = 64
EXPERTS = 16
ROWS_INFO = 40
F32 = jnp.float32
BF16 = jnp.bfloat16


def position():
    dp, expert = lax.axis_index("dp"), lax.axis_index("expert")
    return dp // 2, dp % 2, expert // SIDE, expert % SIDE


def place(z, core, x, y, dz=0, dx=0, dy=0, nz=1, other=False):
    zz = lax.rem(z + dz + nz, nz) if dz else z
    cc = 1 - core if other else core
    xx = lax.rem(x + dx + SIDE, SIDE)
    yy = lax.rem(y + dy + SIDE, SIDE)
    return {"dp": zz * 2 + cc, "expert": xx * SIDE + yy}


def remote(src, dst, send, recv, device):
    return pltpu.make_async_remote_copy(
        src_ref=src, dst_ref=dst, send_sem=send, recv_sem=recv, device_id=device, device_id_type=MESH
    )


def meet(devices):
    barrier = pltpu.get_barrier_semaphore()
    for device in devices:
        pl.semaphore_signal(barrier, inc=1, device_id=device, device_id_type=MESH)
    pl.semaphore_wait(barrier, len(devices))


def hot_rows(rank_row):
    rows = lax.broadcasted_iota(jnp.int32, (CAP, rank_row.shape[1]), 0).astype(F32)
    return rank_row == rows


def rank_row(infos, f, d, x, y, ef, ed):
    expert = lax.rem(x + ed, SIDE) * SIDE + lax.rem(y + ef, SIDE)
    return infos[f, d, pl.ds(expert, 1), :]


def selection(infos, half, step, x, y):
    parts = []
    for other in range(SIDE):
        if half == 0:
            row = rank_row(infos, 0, step, x, y, other, 0)
        else:
            row = rank_row(infos, step, 0, x, y, 0, other)
        parts.append(hot_rows(row))
    return jnp.where(jnp.concatenate(parts, axis=0), 1.0, 0.0).astype(BF16)


class Dispatch:
    def __init__(self, source, wide, sent, rows, s1, r1, s2, r2, here):
        self.source, self.wide, self.sent, self.rows = source, wide, sent, rows
        self.s1, self.r1, self.s2, self.r2 = s1, r1, s2, r2
        self.here = here
        self.width = source.shape[1] // 2

    def peer(self, half, step):
        return place(*self.here, dx=step) if half == 0 else place(*self.here, dy=step)

    def first(self, half, step):
        src = self.source.at[:, pl.ds(half * self.width, self.width)]
        return remote(
            src, self.wide.at[half, step - 1], self.s1.at[half, step - 1], self.r1.at[half, step - 1],
            self.peer(half, step),
        )

    def second(self, half, f, d):
        hop = f if half == 0 else d
        return remote(
            self.sent.at[half, f, d], self.rows.at[half, f, d], self.s2.at[half, f, d], self.r2.at[half, f, d],
            self.peer(1 - half, hop),
        )

    def start(self):
        for step in (2, 1, 3):
            for half in range(2):
                self.first(half, step).start()

    def forward(self, infos, half, step):
        _, _, x, y = self.here
        if step:
            self.first(half, step).wait_recv()
            block = self.wide[half, step - 1]
        else:
            block = self.source[:, half * self.width : (half + 1) * self.width]
        picked = jnp.dot(selection(infos, half, step, x, y), block, preferred_element_type=F32)
        for hop in (2, 1, 3, 0):
            f, d = (hop, step) if half == 0 else (step, hop)
            value = picked[hop * CAP : (hop + 1) * CAP].astype(BF16)
            if hop:
                self.sent[half, f, d] = value
                self.second(half, f, d).start()
            else:
                self.rows[half, f, d] = value

    def arrived(self, f):
        for d in range(SIDE):
            if f:
                self.second(0, f, d).wait_recv()
            if d:
                self.second(1, f, d).wait_recv()

    def finish(self):
        for half in range(2):
            for step in range(1, SIDE):
                self.first(half, step).wait_send()
            for a in range(SIDE):
                for hop in range(1, SIDE):
                    f, d = (hop, a) if half == 0 else (a, hop)
                    self.second(half, f, d).wait_send()


def forward_kernel(
    nz, tokens, targets, info, seq_column, w_gate, w_up, w_down,
    mixed, error_low, hidden, infos, partial,
    down, wide, sent, rows, outs, back, part_out, part_in,
    i_s, i_r, s1, r1, s2, r2, w_s, w_r, b_s, b_r, p_s, p_r,
):
    here = position()
    z, core, x, y = here
    width = tokens.shape[1] // 2
    ring = lambda dz: place(*here, dz=dz, nz=nz)
    peers = [place(*here, dx=step) for step in range(1, SIDE)] + [place(*here, dy=step) for step in range(1, SIDE)]
    peers.append(place(*here, other=True, nz=nz))
    if nz > 1:
        peers += [ring(1), ring(-1)]
    meet(peers)

    infos[0, 0] = info[...]

    def info_x(step):
        return remote(info, infos.at[0, step], i_s.at[0, step - 1], i_r.at[0, step - 1], place(*here, dx=step))

    def info_y(step):
        return remote(infos.at[0], infos.at[step], i_s.at[1, step - 1], i_r.at[1, step - 1], place(*here, dy=step))

    for step in range(1, SIDE):
        info_x(step).start()
    go = Dispatch(tokens, wide, sent, rows, s1, r1, s2, r2, here)
    go.start()

    ups, downs = nz // 2, nz - 1 - nz // 2

    def gather(way, step):
        block = lax.rem(z - step + nz, nz) if way == 0 else lax.rem(z + step, nz)
        ref = down.at[block, core]
        src = w_down if step == 0 else ref
        return remote(src, ref, w_s.at[way, step], w_r.at[way, step], ring(1 if way == 0 else -1))

    down[z, core] = w_down[...]

    def gather_step(step):
        for way, count in ((0, ups), (1, downs)):
            if 0 < step <= count:
                gather(way, step - 1).wait_recv()
            if step < count:
                gather(way, step).start()

    gather_step(0)
    for step in range(1, SIDE):
        info_x(step).wait_recv()
    for step in range(1, SIDE):
        info_y(step).start()
    go.forward(infos, 0, 0)
    gather_step(1)
    for step in range(1, SIDE):
        info_y(step).wait_recv()
    go.forward(infos, 1, 0)
    gather_step(2)
    tick = 3
    for step in (1, 3, 2):
        for half in range(2):
            go.forward(infos, half, step)
            gather_step(tick)
            tick += 1
    for step in range(tick, max(ups, downs) + 1):
        gather_step(step)
    twin = remote(down.at[:, core], down.at[:, core], w_s.at[0, ups], w_r.at[0, ups], place(*here, other=True, nz=nz))
    twin.start()
    twin.wait_send()
    twin_in = remote(
        down.at[:, 1 - core], down.at[:, 1 - core], w_s.at[0, ups], w_r.at[0, ups], place(*here, other=True, nz=nz)
    )
    twin_in.wait_recv()

    def home(half, f, d):
        if half == 0:
            return remote(
                outs.at[0, f], back.at[0, f], b_s.at[0, f, 0], b_r.at[0, f, 0], place(*here, dy=-f)
            )
        return remote(outs.at[1, f, d], back.at[1, f, d], b_s.at[1, f, d], b_r.at[1, f, d], place(*here, dx=-d))

    for f in range(SIDE):
        go.arrived(f)
        gate = jnp.zeros((SIDE * CAP, w_gate.shape[1]), F32)
        up = jnp.zeros((SIDE * CAP, w_gate.shape[1]), F32)
        for half in range(2):
            block = rows[half, f].reshape(SIDE * CAP, width)
            gate = gate + jnp.dot(block, w_gate[half * width : (half + 1) * width], preferred_element_type=F32)
            up = up + jnp.dot(block, w_up[half * width : (half + 1) * width], preferred_element_type=F32)
        unit = ((gate / (1.0 + jnp.exp(-gate))) * up).astype(BF16)
        hidden[f] = unit
        weights = []
        for d in range(SIDE):
            own = x * SIDE + y
            ranks, gates = infos[f, d, pl.ds(own, 1), :], infos[f, d, pl.ds(own + EXPERTS, 1), :]
            weights.append(jnp.sum(jnp.where(hot_rows(ranks), gates, 0.0), axis=1, keepdims=True))
        weight = jnp.concatenate(weights, axis=0)
        for half in range(2):
            matrix = down[half * nz // 2 : (half + 1) * nz // 2].reshape(width, -1)
            value = lax.dot_general(unit, matrix, (((1,), (1,)), ((), ())), preferred_element_type=F32)
            value = (value * weight).astype(BF16).reshape(SIDE, CAP, width)
            if half == 0:
                if f:
                    outs[0, f] = value
                    home(0, f, 0).start()
                else:
                    back[0, 0] = value
            else:
                for d in range(SIDE):
                    if d:
                        outs[1, f, d] = value[d]
                        home(1, f, d).start()
                    else:
                        back[1, f, 0] = value[0]

    def share(half, step):
        device = place(*here, dx=-step) if half == 0 else place(*here, dy=-step)
        return remote(
            part_out.at[half, step - 1], part_in.at[half, step - 1], p_s.at[half, step - 1], p_r.at[half, step - 1], device
        )

    own_parts = []
    for half in range(2):
        if half == 0:
            for f in range(1, SIDE):
                home(0, f, 0).wait_recv()
        for step in (2, 1, 3, 0):
            if half == 0:
                block = back[0, :, step].reshape(SIDE * CAP, width)
            else:
                for d in range(1, SIDE):
                    home(1, step, d).wait_recv()
                block = back[1, step].reshape(SIDE * CAP, width)
            total = lax.dot_general(
                selection(infos, half, step, x, y), block, (((0,), (0,)), ((), ())), preferred_element_type=F32
            )
            if step:
                part_out[half, step - 1] = total.astype(BF16)
                share(half, step).start()
            else:
                own_parts.append(total)
    squares = jnp.zeros((tokens.shape[0], 1), F32)
    for half in range(2):
        total = own_parts[half]
        for step in range(1, SIDE):
            share(half, step).wait_recv()
            total = total + part_in[half, step - 1].astype(F32)
        columns = slice(half * width, (half + 1) * width)
        mixed[:, columns] = total.astype(BF16)
        error = total - targets[:, columns].astype(F32)
        error_low[:, columns] = error.astype(BF16)
        squares = squares + jnp.sum(error * error, axis=1, keepdims=True)
    lane = lax.broadcasted_iota(jnp.int32, (tokens.shape[0], 2 * NSEQ), 1)
    number = jnp.where(lane < NSEQ, lane, lane - NSEQ)
    entry = jnp.where(lane < NSEQ, squares, 1.0)
    sums = jnp.sum(jnp.where(seq_column[...] == number, entry, 0.0), axis=0, keepdims=True)
    partial[...] = jnp.broadcast_to(sums, partial.shape)

    go.finish()
    for step in range(1, SIDE):
        info_x(step).wait_send()
        info_y(step).wait_send()
        share(0, step).wait_send()
        share(1, step).wait_send()
        home(0, step, 0).wait_send()
        for f in range(SIDE):
            home(1, f, step).wait_send()
    for way, count in ((0, ups), (1, downs)):
        for step in range(count):
            gather(way, step).wait_send()


def dual_search(loss_column):
    lane = lax.broadcasted_iota(jnp.int32, (1, 128), 1).astype(F32)
    upper = jnp.sum(loss_column, axis=0, keepdims=True)
    lower = -upper
    for bits in (7, 7, 7, 7, 7, 5):
        ways = float(2**bits)
        width = (upper - lower) / ways
        middle = lower + width * (lane + 1.0)
        excess = jnp.maximum(loss_column - middle, 0.0)
        plain = jnp.sum(excess, axis=0, keepdims=True)
        square = jnp.sum(excess * excess, axis=0, keepdims=True)
        below = (NSEQ * square - 2.0 * plain * plain < 0.0) & (lane < ways - 1.0)
        count = jnp.sum(jnp.where(below, 1.0, 0.0), axis=1, keepdims=True)
        lower, upper = lower + width * count, lower + width * (count + 1.0)
    return 0.5 * (lower + upper)


def backward_kernel(
    nz, scale, features, error, hidden, infos, partial,
    grad, losses,
    wide, sent, rows, total, seen, grads, twin_in, ring_out, ring_in,
    s1, r1, s2, r2, a_s, a_r, t_s, t_r, g_s, g_r,
):
    here = position()
    z, core, x, y = here
    width = error.shape[1] // 2
    ring = lambda dz: place(*here, dz=dz, nz=nz)
    peers = [place(*here, dx=step) for step in range(1, SIDE)] + [place(*here, dy=step) for step in range(1, SIDE)]
    peers.append(place(*here, other=True, nz=nz))
    strides = []
    stride = 1
    while stride < nz:
        strides.append(stride)
        stride *= 2

    def across(stride):
        bit = lax.rem(z // stride, 2)
        return {"dp": (z + stride - 2 * stride * bit) * 2 + core, "expert": x * SIDE + y}

    for stride in strides:
        peers.append(across(stride))
    if nz > 1:
        peers += [ring(1), ring(-1)]
    meet(peers)

    go = Dispatch(error, wide, sent, rows, s1, r1, s2, r2, here)
    go.start()

    stages = [
        [place(*here, dx=step) for step in range(1, SIDE)],
        [place(*here, dy=step) for step in range(1, SIDE)],
        [place(*here, other=True, nz=nz)],
    ] + [[across(stride)] for stride in strides]
    total[0] = partial[...]

    def tell(stage, index):
        return remote(
            total.at[stage], seen.at[stage, index], a_s.at[stage, index], a_r.at[stage, index], stages[stage][index]
        )

    def stage_start(stage):
        for index in range(len(stages[stage])):
            tell(stage, index).start()

    def stage_end(stage):
        value = total[stage]
        for index in range(len(stages[stage])):
            tell(stage, index).wait_recv()
            value = value + seen[stage, index]
        total[stage + 1] = value
        if stage + 1 < len(stages):
            stage_start(stage + 1)

    stage_start(0)
    done = 0
    for step in (0, 1, 3, 2):
        for half in range(2):
            go.forward(infos, half, step)
            if done < len(stages):
                stage_end(done)
                done += 1
    while done < len(stages):
        stage_end(done)
        done += 1

    sums = total[len(stages)][0:1]
    lengths = pltpu.roll(sums, NSEQ, 1)
    loss_row = sums / (lengths * float(features))
    eye = lax.broadcasted_iota(jnp.int32, (NSEQ, 128), 0) == lax.broadcasted_iota(jnp.int32, (NSEQ, 128), 1)
    column = lambda row: jnp.sum(jnp.where(eye, row, 0.0), axis=1, keepdims=True)
    loss_column = column(loss_row)
    eta = dual_search(loss_column)
    excess_column = jnp.maximum(loss_column - eta, 0.0)
    norm = jnp.sum(excess_column, axis=0, keepdims=True)
    dual_row = jnp.maximum(loss_row - eta, 0.0) / norm
    losses[0:1, :] = loss_row
    losses[1:2, :] = dual_row
    rate = (excess_column / norm) / column(lengths)

    own = x * SIDE + y
    numbers = lax.broadcasted_iota(jnp.int32, (NSEQ, 128), 0).astype(F32)
    scaled = []
    for f in range(SIDE):
        weights = []
        for d in range(SIDE):
            ranks, gates = infos[f, d, pl.ds(own, 1), :], infos[f, d, pl.ds(own + EXPERTS, 1), :]
            seq_row = infos[f, d, 2 * EXPERTS : 2 * EXPERTS + 1, :]
            token_rate = jnp.sum(jnp.where(seq_row == numbers, rate, 0.0), axis=0, keepdims=True)
            token_weight = (scale * gates) * token_rate
            weights.append(jnp.sum(jnp.where(hot_rows(ranks), token_weight, 0.0), axis=1, keepdims=True))
        weight = jnp.concatenate(weights, axis=0)
        scaled.append((hidden[f].astype(F32) * weight).astype(BF16))
    scaled = jnp.concatenate(scaled, axis=0)

    for f in range(SIDE):
        go.arrived(f)
    block = 64
    chunk = 4 * block * 2
    for half in range(2):
        for part in range(width // chunk):
            value = lax.dot_general(
                rows[half, :, :, :, part * chunk : (part + 1) * chunk].reshape(SIDE * SIDE * CAP, chunk),
                scaled, (((0,), (0,)), ((), ())), preferred_element_type=F32,
            )
            first = (half * width + part * chunk) // (2 * block)
            grads[first : first + chunk // (2 * block)] = value.reshape(chunk // (2 * block), 2, block, -1)

    twin = remote(grads.at[:, 1 - core], twin_in, t_s, t_r, place(*here, other=True, nz=nz))
    twin.start()
    twin.wait_recv()

    def own_part(target):
        return grads[target, core] + twin_in[target]

    ups, downs = nz // 2 - 1, nz // 2

    def pass_on(way, step):
        return remote(
            ring_out.at[way, step], ring_in.at[way, step], g_s.at[way, step], g_r.at[way, step],
            ring(1 if way == 0 else -1),
        )

    for step in range(downs):
        for way, count in ((0, ups), (1, downs)):
            if step < count:
                target = lax.rem(z + count - step, nz) if way == 0 else lax.rem(z - count + step + nz, nz)
                value = own_part(target)
                if step:
                    pass_on(way, step - 1).wait_recv()
                    value = value + ring_in[way, step - 1]
                ring_out[way, step] = value
                pass_on(way, step).start()
    value = own_part(z)
    for way, count in ((0, ups), (1, downs)):
        if count:
            pass_on(way, count - 1).wait_recv()
            value = value + ring_in[way, count - 1]
    grad[...] = value

    go.finish()
    twin.wait_send()
    for way, count in ((0, ups), (1, downs)):
        for step in range(count):
            pass_on(way, step).wait_send()
    for stage in range(len(stages)):
        for index in range(len(stages[stage])):
            tell(stage, index).wait_send()


def local(nz, tokens, targets, routes, route_logits, slot_order, seq_ids, w_gate, w_up, w_down):
    tok, feat = tokens.shape
    top = routes.shape[1]
    units = w_gate.shape[2]
    scale = float(tok * lax.axis_size("dp") * lax.axis_size("expert") // 8)
    width = feat // 2

    routes_t, logits_t, order_t = routes.T, route_logits.T, slot_order.T
    slots = lax.broadcasted_iota(jnp.int32, (1, top, 1), 1)
    picked = jnp.sum(jnp.where(order_t[:, None, :] == slots, logits_t[None, :, :], 0.0), axis=1)
    raised = jnp.exp(picked)
    gates = raised / jnp.sum(raised, axis=0, keepdims=True)
    hot = routes_t[None, :, :] == lax.broadcasted_iota(jnp.int32, (EXPERTS, 1, 1), 0)
    named = jnp.sum(jnp.where(hot, 1.0, 0.0), axis=1)
    gate_of = jnp.sum(jnp.where(hot, gates[None], 0.0), axis=1)
    earlier = lax.broadcasted_iota(jnp.int32, (tok, tok), 0) < lax.broadcasted_iota(jnp.int32, (tok, tok), 1)
    ranks = jnp.dot(named.astype(BF16), earlier.astype(BF16), preferred_element_type=F32)
    ranks = jnp.where(named > 0.5, ranks, -1.0)
    seq_rows = jnp.broadcast_to(seq_ids.astype(F32)[None, :], (ROWS_INFO - 2 * EXPERTS, tok))
    info = jnp.concatenate([ranks, gate_of, seq_rows], axis=0)

    vmem = pl.BlockSpec(memory_space=pltpu.VMEM)
    dma = pltpu.SemaphoreType.DMA
    travel = [
        pltpu.VMEM((2, SIDE - 1, tok, width), BF16),
        pltpu.VMEM((2, SIDE, SIDE, CAP, width), BF16),
        pltpu.VMEM((2, SIDE, SIDE, CAP, width), BF16),
    ]
    travel_sems = [
        dma((2, SIDE - 1)), dma((2, SIDE - 1)), dma((2, SIDE, SIDE)), dma((2, SIDE, SIDE)),
    ]
    flops = 2 * EXPERTS * CAP * feat * units
    mixed, error_low, hidden, infos, partial = pl.pallas_call(
        functools.partial(forward_kernel, nz),
        out_shape=(
            jax.ShapeDtypeStruct((tok, feat), BF16),
            jax.ShapeDtypeStruct((tok, feat), BF16),
            jax.ShapeDtypeStruct((SIDE, SIDE * CAP, units), BF16),
            jax.ShapeDtypeStruct((SIDE, SIDE, ROWS_INFO, tok), F32),
            jax.ShapeDtypeStruct((8, 128), F32),
        ),
        in_specs=[vmem] * 7,
        out_specs=[vmem] * 5,
        scratch_shapes=[
            pltpu.VMEM((nz, 2, feat // (2 * nz), units), BF16),
            *travel,
            pltpu.VMEM((2, SIDE, SIDE, CAP, width), BF16),
            pltpu.VMEM((2, SIDE, SIDE, CAP, width), BF16),
            pltpu.VMEM((2, SIDE - 1, tok, width), BF16),
            pltpu.VMEM((2, SIDE - 1, tok, width), BF16),
            dma((2, SIDE - 1)), dma((2, SIDE - 1)),
            *travel_sems,
            dma((2, nz // 2 + 1)), dma((2, nz // 2 + 1)),
            dma((2, SIDE, SIDE)), dma((2, SIDE, SIDE)),
            dma((2, SIDE - 1)), dma((2, SIDE - 1)),
        ],
        compiler_params=pltpu.CompilerParams(
            collective_id=0, has_side_effects=True, vmem_limit_bytes=56 * 2**20
        ),
        cost_estimate=pl.CostEstimate(flops=3 * flops, bytes_accessed=8 * 2**20, transcendentals=0),
        name="forward",
    )(tokens, targets, info, seq_ids[:, None], w_gate[0], w_up[0], w_down[:, 0])

    block = feat // (2 * nz)
    stages = 3 + (nz - 1).bit_length()
    grad, losses = pl.pallas_call(
        functools.partial(backward_kernel, nz, scale, feat),
        out_shape=(
            jax.ShapeDtypeStruct((block, units), F32),
            jax.ShapeDtypeStruct((8, 128), F32),
        ),
        in_specs=[vmem] * 4,
        out_specs=[vmem] * 2,
        scratch_shapes=[
            *travel,
            pltpu.VMEM((stages + 1, 8, 128), F32),
            pltpu.VMEM((stages, SIDE - 1, 8, 128), F32),
            pltpu.VMEM((nz, 2, block, units), F32),
            pltpu.VMEM((nz, block, units), F32),
            pltpu.VMEM((2, nz // 2, block, units), F32),
            pltpu.VMEM((2, nz // 2, block, units), F32),
            *travel_sems,
            dma((stages, SIDE - 1)), dma((stages, SIDE - 1)),
            dma, dma,
            dma((2, nz // 2)), dma((2, nz // 2)),
        ],
        compiler_params=pltpu.CompilerParams(
            collective_id=1, has_side_effects=True, vmem_limit_bytes=56 * 2**20
        ),
        cost_estimate=pl.CostEstimate(flops=flops, bytes_accessed=8 * 2**20, transcendentals=0),
        name="backward",
    )(error_low, hidden, infos, partial)
    return (mixed, losses[0, :NSEQ], losses[1, :NSEQ], grad[:, None, :])


def solution(mesh):
    return jax.shard_map(
        functools.partial(local, mesh.shape["dp"] // 2),
        mesh=mesh,
        in_specs=(
            P(("dp", "expert"), None),
            P(("dp", "expert"), None),
            P(("dp", "expert"), None),
            P(("dp", "expert"), None),
            P(("dp", "expert"), None),
            P(("dp", "expert")),
            P("expert", None, None),
            P("expert", None, None),
            P("dp", "expert", None),
        ),
        out_specs=(P(("dp", "expert"), None), P(), P(), P("dp", "expert", None)),
        check_vma=False,
    )
```

time: 802 us -> 201 us (0.25)
  waiting for transfers between devices: 397 us -> 0 us
  Pallas kernels: 0 us -> 192 us
  loops' own time: 147 us -> 0 us
  blocking collectives: 107 us -> 0 us
  local copies, waits for them, and re-layouts: 47 us -> 5.09 us
  other arithmetic: 40.3 us -> 2.75 us
  starting transfers between devices: 24.3 us -> 0 us
  matrix products: 20.8 us -> 0.14 us
  between operations: 16.2 us -> 0.67 us
    unnamed x3 -> x0, waiting for transfers between devices: 221 us -> none
    pallas_call x0 -> x2, Pallas kernels: none -> 192 us  [the longest x1 107 us: local(): pl.pallas_call(functools.partial(forward_kernel, nz), out_shape=(jax.Shap...]
    all_to_all x4 -> x0, waiting for transfers between devices: 152 us -> none  [the longest x1 55.6 us: local(): lax.all_to_all(by_source(expert_out, groups), 'expert', split_axis=0, con...]
    another operation x1 -> x0, loops' own time: 147 us -> none  [dual_search(): lax.fori_loop(0, BISECT_STEPS, advance, (-sum_total, sum_total))]
    psum x1 -> x0, blocking collectives: 107 us -> none  [local(): seq_sq, seq_len = lax.psum((partial_sq, counts), ('dp', 'expert'))]
    reduce_sum x48 -> x3, other arithmetic: 32.1 us -> 1.47 us  [the longest x1 0.73 us: local(): named = jnp.sum(jnp.where(hot, 1.0, 0.0), axis=1)]
    gather x4 -> x0, local copies, waits for them, and re-layouts: 28.1 us -> none  [the longest x1 11.6 us: local(): returned.reshape(slot_count, feat_width)[slot_index]]
    all_to_all x4 -> x0, starting transfers between devices: 24.2 us -> none  [the longest x1 7.64 us: local(): lax.all_to_all(send_rows, 'expert', split_axis=0, concat_axis=0, tiled=True)]
  transfers between devices with their start and end apart: 6 -> 0, of which waited for: 6 -> 0; matrix products, arithmetic and copies ran while one was open for 2% -> 0% of each run, Pallas kernels for 0% -> 0%
where the time goes in v1:
time: 201 us; the launch traced here: 200 us
  Pallas kernels  192 us (96%)
  local copies, waits for them, and re-layouts  5.09 us (3%)
  other arithmetic  2.75 us (1%)
    pallas_call x1, Pallas kernels, local(): pl.pallas_call(functools.partial(forward_kernel, nz), out_shape=(jax.Shap...  107 us
    pallas_call x1, Pallas kernels, local(): pl.pallas_call(functools.partial(backward_kernel, nz, scale, feat), out_s...  85 us

profile of v1, /device:TPU:1, one launch (start us, length us, event | category | flops | bytes accessed | tf_op | source)
XLA Modules:
  0.0 200.4 jit_solution(5186119242533223012)
XLA Ops:
  0.6 0.7 select_reduce_fusion.2
  1.4 0.7 select_reduce_fusion.1
  2.1 0.1 convolution_select_fusion
  2.3 0.7 convert_element_type.8
  2.9 0.6 pad_maximum_fusion.info
  3.5 1.4 copy.15.seq_column
  4.9 106.7 %forward.1 = (bf16[128,2048]{1,0:T(8,128)(2,1)}, bf16[128,2048]{1,0:T(8,128)(2,1)}, bf16[4,256,384]{2,1,0:T(8,128)(2,1)}, f32[4,4,40,128]{3,2,1,0:T(8,128)}, f32[8,128]{1,0:T(8,128)}) custom-call(bf16[128,2048]{1,0:T(8,128)(2,1)} %tokens.1, bf16[128,2048]{1,0:T(8,128)(2,1)} %targets.1, f32[40,128]{1,0:T(8,128)} %pad_maximum_fusion.info, ...), custom_call_target="tpu_custom_call" | custom-call | flops 4831838208 | bytes 8388608 | tf_op jit(solution)/shard_map/forward/pallas_call | solution.py:502
  111.6 0.0 copy-start
  111.6 85.0 %backward.1 = (f32[64,384]{1,0:T(8,128)}, f32[8,128]{1,0:T(8,128)}) custom-call(bf16[128,2048]{1,0:T(8,128)(2,1)} %get-tuple-element.12.error, bf16[4,256,384]{2,1,0:T(8,128)(2,1)} %get-tuple-element.13.hidden, f32[4,4,40,128]{3,2,1,0:T(8,128)} %get-tuple-element.14.infos, f32[8,128]{1,0:T(8,128)} %get-tuple-element.15.partial), custom_call_target="tpu_custom_call" | custom-call | flops 1610612736 | bytes 8388608 | tf_op jit(solution)/shard_map/backward/pallas_call | solution.py:535
  196.7 1.3 slice_bitcast_fusion
  198.0 1.6 copy.16
  199.6 0.0 copy-done
  199.6 0.8 copy.18
  (3 shorter events, 0.0 us)
Async XLA Ops:
  111.6 88.0 %copy-start = (bf16[128,2048]{1,0:T(8,128)(2,1)S(1)}, bf16[128,2048]{1,0:T(8,128)(2,1)}, u32[]{:S(2)}) copy-start(bf16[128,2048]{1,0:T(8,128)(2,1)} %get-tuple-element.34) | copy-start | bytes 1572868

commit v2 on v1

v2 whole, which is shorter than its diff:
```python
import functools

import jax
import jax.numpy as jnp
from jax import lax
from jax.experimental import pallas as pl
from jax.experimental.pallas import tpu as pltpu
from jax.sharding import PartitionSpec as P

MESH = pl.DeviceIdType.MESH
SIDE = 4
NSEQ = 64
CAP = 64
EXPERTS = 16
ROWS_INFO = 40
PASSES = 4
CUTS = 4
LANES = 128
F32 = jnp.float32
BF16 = jnp.bfloat16


def position():
    dp, expert = lax.axis_index("dp"), lax.axis_index("expert")
    return dp // 2, dp % 2, expert // SIDE, expert % SIDE


def place(z, core, x, y, dz=0, dx=0, dy=0, nz=1, other=False):
    zz = lax.rem(z + dz + nz, nz) if dz else z
    cc = 1 - core if other else core
    xx = lax.rem(x + dx + SIDE, SIDE)
    yy = lax.rem(y + dy + SIDE, SIDE)
    return {"dp": zz * 2 + cc, "expert": xx * SIDE + yy}


def remote(src, dst, send, recv, device):
    return pltpu.make_async_remote_copy(
        src_ref=src, dst_ref=dst, send_sem=send, recv_sem=recv, device_id=device, device_id_type=MESH
    )


def meet(devices):
    barrier = pltpu.get_barrier_semaphore()
    for device in devices:
        pl.semaphore_signal(barrier, inc=1, device_id=device, device_id_type=MESH)
    pl.semaphore_wait(barrier, len(devices))


def hot_rows(rank_row):
    rows = lax.broadcasted_iota(jnp.int32, (CAP, rank_row.shape[1]), 0).astype(F32)
    return rank_row == rows


def rank_row(infos, f, d, x, y, ef, ed):
    expert = lax.rem(x + ed, SIDE) * SIDE + lax.rem(y + ef, SIDE)
    return infos[f, d, pl.ds(expert, 1), :]


def selection(infos, half, step, x, y):
    parts = []
    for other in range(SIDE):
        if half == 0:
            row = rank_row(infos, 0, step, x, y, other, 0)
        else:
            row = rank_row(infos, step, 0, x, y, 0, other)
        parts.append(hot_rows(row))
    return jnp.where(jnp.concatenate(parts, axis=0), 1.0, 0.0).astype(BF16)


class Dispatch:
    def __init__(self, source, wide, sent, rows, s1, r1, s2, r2, here):
        self.source, self.wide, self.sent, self.rows = source, wide, sent, rows
        self.s1, self.r1, self.s2, self.r2 = s1, r1, s2, r2
        self.here = here
        self.width = source.shape[1] // 2

    def peer(self, half, step):
        return place(*self.here, dx=step) if half == 0 else place(*self.here, dy=step)

    def first(self, half, step):
        src = self.source.at[:, pl.ds(half * self.width, self.width)]
        return remote(
            src, self.wide.at[half, step - 1], self.s1.at[half, step - 1], self.r1.at[half, step - 1],
            self.peer(half, step),
        )

    def second(self, half, f, d):
        hop = f if half == 0 else d
        return remote(
            self.sent.at[half, f, d], self.rows.at[half, f, d], self.s2.at[half, f, d], self.r2.at[half, f, d],
            self.peer(1 - half, hop),
        )

    def start(self):
        for step in (2, 1, 3):
            for half in range(2):
                self.first(half, step).start()

    def forward(self, infos, half, step, send=True):
        _, _, x, y = self.here
        if step:
            self.first(half, step).wait_recv()
            block = self.wide[half, step - 1]
        else:
            block = self.source[:, half * self.width : (half + 1) * self.width]
        picked = jnp.dot(selection(infos, half, step, x, y), block, preferred_element_type=F32)
        for hop in (2, 1, 3, 0):
            f, d = (hop, step) if half == 0 else (step, hop)
            value = picked[hop * CAP : (hop + 1) * CAP].astype(BF16)
            if hop:
                self.sent[half, f, d] = value
                if send:
                    self.second(half, f, d).start()
            else:
                self.rows[half, f, d] = value

    def arrived(self, f):
        for d in range(SIDE):
            if f:
                self.second(0, f, d).wait_recv()
            if d:
                self.second(1, f, d).wait_recv()

    def finish(self):
        for half in range(2):
            for step in range(1, SIDE):
                self.first(half, step).wait_send()
            for a in range(SIDE):
                for hop in range(1, SIDE):
                    f, d = (hop, a) if half == 0 else (a, hop)
                    self.second(half, f, d).wait_send()


def dual_search(loss_column):
    lane = lax.broadcasted_iota(jnp.int32, (1, 128), 1).astype(F32)
    upper = jnp.sum(loss_column, axis=0, keepdims=True)
    lower = -upper
    for bits in (7, 7, 7, 7, 7, 5):
        ways = float(2**bits)
        width = (upper - lower) / ways
        middle = lower + width * (lane + 1.0)
        excess = jnp.maximum(loss_column - middle, 0.0)
        plain = jnp.sum(excess, axis=0, keepdims=True)
        square = jnp.sum(excess * excess, axis=0, keepdims=True)
        below = (NSEQ * square - 2.0 * plain * plain < 0.0) & (lane < ways - 1.0)
        count = jnp.sum(jnp.where(below, 1.0, 0.0), axis=1, keepdims=True)
        lower, upper = lower + width * count, lower + width * (count + 1.0)
    return 0.5 * (lower + upper)


def sums_over(infos, f, d, own, values=None):
    ranks, gates = infos[f, d, pl.ds(own, 1), :], infos[f, d, pl.ds(own + EXPERTS, 1), :]
    entry = gates if values is None else values(f, d, gates)
    return jnp.sum(jnp.where(hot_rows(ranks), entry, 0.0), axis=1, keepdims=True)


def column_of(row, size):
    shape = (size, row.shape[1])
    eye = lax.broadcasted_iota(jnp.int32, shape, 0) == lax.broadcasted_iota(jnp.int32, shape, 1)
    return jnp.sum(jnp.where(eye, row, 0.0), axis=1, keepdims=True)


def step_kernel(
    nz, scale, tokens, targets, info, w_gate, w_up, w_down,
    mixed, grad, losses,
    infos, hidden, down, wide, sent, rows, outs, back, part_out, part_in,
    err, err_wide, err_sent, err_rows, seen, grads, twin_in, ring_out, ring_in,
    i_s, i_r, s1, r1, s2, r2, w_s, w_r, b_s, b_r, p_s, p_r,
    e1s, e1r, e2s, e2r, a_s, a_r, t_s, t_r, g_s, g_r,
):
    here = position()
    z, core, x, y = here
    tok, feat = tokens.shape
    width = feat // 2
    own = x * SIDE + y
    ring = lambda dz: place(*here, dz=dz, nz=nz)
    twin_device = place(*here, other=True)
    low, high = z % SIDE, z // SIDE
    around = lambda index, step, size: lax.rem(index + step, size)
    stage_sizes = (SIDE, 2 * SIDE, SIDE, SIDE)
    stage_index = (x, y * 2 + core, low, high)

    def stage_device(stage, step):
        if stage == 0:
            return place(*here, dx=step)
        if stage == 1:
            to = around(y * 2 + core, step, 2 * SIDE)
            return {"dp": z * 2 + to % 2, "expert": x * SIDE + to // 2}
        if stage == 2:
            return {"dp": (high * SIDE + around(low, step, SIDE)) * 2 + core, "expert": own}
        return {"dp": (around(high, step, SIDE) * SIDE + low) * 2 + core, "expert": own}

    peers = [stage_device(stage, step) for stage in range(4) for step in range(1, stage_sizes[stage])]
    peers += [ring(1), ring(-1)]
    meet(peers)

    infos[0, 0] = info[...]

    def info_x(step):
        return remote(info, infos.at[0, step], i_s.at[0, step - 1], i_r.at[0, step - 1], place(*here, dx=step))

    def info_y(step):
        return remote(infos.at[0], infos.at[step], i_s.at[1, step - 1], i_r.at[1, step - 1], place(*here, dy=step))

    for step in range(1, SIDE):
        info_x(step).start()
    go = Dispatch(tokens, wide, sent, rows, s1, r1, s2, r2, here)
    go.start()

    ups, downs = nz // 2, nz - 1 - nz // 2

    def gather(way, step):
        block = lax.rem(z - step + nz, nz) if way == 0 else lax.rem(z + step, nz)
        ref = down.at[block, core]
        src = w_down if step == 0 else ref
        return remote(src, ref, w_s.at[way, step], w_r.at[way, step], ring(1 if way == 0 else -1))

    down[z, core] = w_down[...]

    def gather_step(step):
        for way, count in ((0, ups), (1, downs)):
            if 0 < step <= count:
                gather(way, step - 1).wait_recv()
            if step < count:
                gather(way, step).start()

    gather_step(0)
    go.forward(infos, 1, 0)
    go.forward(infos, 0, 0, send=False)
    gather_step(1)
    for step in range(1, SIDE):
        info_x(step).wait_recv()
    for step in range(1, SIDE):
        info_y(step).start()
    gather_step(2)
    tick = 3
    for step in (1, 3, 2):
        go.forward(infos, 0, step, send=False)
        gather_step(tick)
        tick += 1
    for step in range(1, SIDE):
        info_y(step).wait_recv()
    for f in (1, 3, 2):
        for d in range(SIDE):
            go.second(0, f, d).start()
        go.forward(infos, 1, f)
        gather_step(tick)
        tick += 1
    for step in range(tick, max(ups, downs) + 1):
        gather_step(step)
    twin_down = [
        remote(down.at[:, side], down.at[:, side], w_s.at[0, ups], w_r.at[0, ups], twin_device) for side in (core, 1 - core)
    ]
    twin_down[0].start()

    def home(half, f, d):
        if half == 0:
            return remote(outs.at[0, f], back.at[0, f], b_s.at[0, f, 0], b_r.at[0, f, 0], place(*here, dy=-f))
        return remote(outs.at[1, f, d], back.at[1, f, d], b_s.at[1, f, d], b_r.at[1, f, d], place(*here, dx=-d))

    def expert(f):
        go.arrived(f)
        gate = jnp.zeros((SIDE * CAP, w_gate.shape[1]), F32)
        up = jnp.zeros((SIDE * CAP, w_gate.shape[1]), F32)
        for half in range(2):
            block = rows[half, f].reshape(SIDE * CAP, width)
            gate = gate + jnp.dot(block, w_gate[half * width : (half + 1) * width], preferred_element_type=F32)
            up = up + jnp.dot(block, w_up[half * width : (half + 1) * width], preferred_element_type=F32)
        unit = ((gate / (1.0 + jnp.exp(-gate))) * up).astype(BF16)
        hidden[f] = unit
        weight = jnp.concatenate([sums_over(infos, f, d, own) for d in range(SIDE)], axis=0)
        if f == 0:
            twin_down[0].wait_send()
            twin_down[1].wait_recv()
        for half in range(2):
            matrix = down[half * nz // 2 : (half + 1) * nz // 2].reshape(width, -1)
            value = lax.dot_general(unit, matrix, (((1,), (1,)), ((), ())), preferred_element_type=F32)
            value = (value * weight).astype(BF16).reshape(SIDE, CAP, width)
            if half == 0:
                if f:
                    outs[0, f] = value
                    home(0, f, 0).start()
                else:
                    back[0, 0] = value
            else:
                for d in range(SIDE):
                    if d:
                        outs[1, f, d] = value[d]
                        home(1, f, d).start()
                    else:
                        back[1, f, 0] = value[0]

    def share(half, step):
        device = place(*here, dx=-step) if half == 0 else place(*here, dy=-step)
        return remote(
            part_out.at[half, step - 1], part_in.at[half, step - 1], p_s.at[half, step - 1], p_r.at[half, step - 1], device
        )

    def merge(half, step):
        if half == 0:
            block = back[0, :, step].reshape(SIDE * CAP, width)
        else:
            for d in range(1, SIDE):
                home(1, step, d).wait_recv()
            block = back[1, step].reshape(SIDE * CAP, width)
        total = lax.dot_general(
            selection(infos, half, step, x, y), block, (((0,), (0,)), ((), ())), preferred_element_type=F32
        )
        if step:
            part_out[half, step - 1] = total.astype(BF16)
            share(half, step).start()
        return total

    expert(0)
    expert(1)
    expert(3)
    merge(1, 1)
    expert(2)
    merge(1, 3)
    for f in range(1, SIDE):
        home(0, f, 0).wait_recv()
    for step in (2, 1, 3):
        merge(0, step)
    merge(1, 2)

    blocks = feat // LANES
    squares = jnp.zeros((tok, 1), F32)
    for half in range(2):
        total = merge(half, 0)
        for step in range(1, SIDE):
            share(half, step).wait_recv()
            total = total + part_in[half, step - 1].astype(F32)
        columns = slice(half * width, (half + 1) * width)
        mixed[:, columns] = total.astype(BF16)
        error = total - targets[:, columns].astype(F32)
        low_error = error.astype(BF16)
        for block in range(width // LANES):
            target = half * (width // LANES) + block
            err[lax.rem(target - z + blocks, blocks)] = low_error[:, block * LANES : (block + 1) * LANES]
        squares = squares + jnp.sum(error * error, axis=1, keepdims=True)
    lane = lax.broadcasted_iota(jnp.int32, (tok, 2 * NSEQ), 1)
    number = jnp.where(lane < NSEQ, lane, lane - NSEQ).astype(F32)
    entry = jnp.where(lane < NSEQ, squares, 1.0)
    seq_column = column_of(info[2 * EXPERTS : 2 * EXPERTS + 1, :], tok)
    partial = jnp.sum(jnp.where(seq_column == number, entry, 0.0), axis=0, keepdims=True)

    def tell(stage, step):
        slot = seen.at[stage, stage_index[stage]]
        return remote(slot, slot, a_s.at[stage, step - 1], a_r.at[stage, step - 1], stage_device(stage, step))

    def stage_start(stage, value):
        seen[stage, stage_index[stage]] = value
        for step in range(1, stage_sizes[stage]):
            tell(stage, step).start()

    def stage_end(stage):
        for step in range(1, stage_sizes[stage]):
            tell(stage, step).wait_recv()
        value = seen[stage, 0]
        for index in range(1, stage_sizes[stage]):
            value = value + seen[stage, index]
        if stage < 3:
            stage_start(stage + 1, value)
        return value

    stage_start(0, jnp.broadcast_to(partial, (8, 2 * NSEQ)))

    per = blocks // (2 * PASSES)

    def span(half, p):
        return blocks // 2 - per * (p + 1) if half == 0 else blocks // 2 + per * p

    def err_first(p, half, step):
        device = place(*here, dx=step) if half == 0 else place(*here, dy=step)
        return remote(
            err.at[pl.ds(span(half, p), per)], err_wide.at[p, half, step - 1],
            e1s.at[p, half, step - 1], e1r.at[p, half, step - 1], device,
        )

    def err_second(p, half, f, d):
        device = place(*here, dy=f) if half == 0 else place(*here, dx=d)
        return remote(
            err_sent.at[p, half, f, d], err_rows.at[p, half, f, d], e2s.at[p, half, f, d], e2r.at[p, half, f, d], device
        )

    def err_start(p):
        for step in (2, 1, 3):
            for half in range(2):
                err_first(p, half, step).start()

    def err_forward(p, half, step):
        if step:
            err_first(p, half, step).wait_recv()
            block = jnp.concatenate([err_wide[p, half, step - 1, i] for i in range(per)], axis=1)
        else:
            block = jnp.concatenate([err[span(half, p) + i] for i in range(per)], axis=1)
        picked = jnp.dot(selection(infos, half, step, x, y), block, preferred_element_type=F32)
        for hop in (2, 1, 3, 0):
            f, d = (hop, step) if half == 0 else (step, hop)
            value = picked[hop * CAP : (hop + 1) * CAP].astype(BF16)
            if hop:
                err_sent[p, half, f, d] = value
                err_second(p, half, f, d).start()
            else:
                err_rows[p, half, f, d] = value

    def err_pass(p):
        for step in (0, 1, 3, 2):
            for half in range(2):
                err_forward(p, half, step)

    def err_arrived(p):
        for half in range(2):
            for a in range(SIDE):
                for hop in range(1, SIDE):
                    f, d = (hop, a) if half == 0 else (a, hop)
                    err_second(p, half, f, d).wait_recv()

    block_rows = LANES // 2

    def twin(p, half):
        ref = pl.ds(span(half, p), per)
        return remote(grads.at[ref, 1 - core], twin_in.at[ref], t_s.at[p, half], t_r.at[p, half], twin_device)

    def gradient(p):
        err_arrived(p)
        for half in range(2):
            value = lax.dot_general(
                err_rows[p, half].reshape(SIDE * SIDE * CAP, per * LANES), scaled,
                (((0,), (0,)), ((), ())), preferred_element_type=F32,
            )
            grads[span(half, p) : span(half, p) + per] = value.reshape(per, 2, block_rows, -1)
            twin(p, half).start()

    cut = block_rows // CUTS
    ring_counts = (blocks // 2 - 1, blocks // 2)

    def pass_on(way, step, k):
        part = pl.ds(k * cut, cut)
        return remote(
            ring_out.at[way, step, part], ring_in.at[way, step, part], g_s.at[way, step, k], g_r.at[way, step, k],
            ring(1 if way == 0 else -1),
        )

    def own_part(block, k):
        part = pl.ds(k * cut, cut)
        return grads[block, core, part] + twin_in[block, part]

    def reduce_steps(p):
        for half in range(2):
            twin(p, half).wait_recv()
        for step in range(per * p, per * (p + 1)):
            for k in range(CUTS):
                for way in range(2):
                    if step < ring_counts[way]:
                        block = blocks // 2 - 1 - step if way == 0 else blocks // 2 + step
                        value = own_part(block, k)
                        if step:
                            pass_on(way, step - 1, k).wait_recv()
                            value = value + ring_in[way, step - 1, pl.ds(k * cut, cut)]
                        ring_out[way, step, pl.ds(k * cut, cut)] = value
                        pass_on(way, step, k).start()

    err_start(0)
    for half in range(2):
        err_forward(0, half, 0)
    err_start(1)
    stage_end(0)
    for stage, step in ((1, 1), (2, 3)):
        for half in range(2):
            err_forward(0, half, step)
        stage_end(stage)
    for half in range(2):
        err_forward(0, half, 2)
    err_start(2)
    err_pass(1)
    sums = stage_end(3)[0:1]
    err_start(3)
    lengths = pltpu.roll(sums, NSEQ, 1)
    loss_row = sums / (lengths * float(feat))
    loss_column = column_of(loss_row, NSEQ)
    eta = dual_search(loss_column)
    excess_column = jnp.maximum(loss_column - eta, 0.0)
    norm = jnp.sum(excess_column, axis=0, keepdims=True)
    losses[0:1, :] = loss_row
    losses[1:2, :] = jnp.maximum(loss_row - eta, 0.0) / norm
    rate = (excess_column / norm) / column_of(lengths, NSEQ)
    numbers = lax.broadcasted_iota(jnp.int32, (NSEQ, tok), 0).astype(F32)

    def token_weights(f, d, gates):
        seq_row = infos[f, d, 2 * EXPERTS : 2 * EXPERTS + 1, :]
        return (scale * gates) * jnp.sum(jnp.where(seq_row == numbers, rate, 0.0), axis=0, keepdims=True)

    scaled = []
    for f in range(SIDE):
        weight = jnp.concatenate([sums_over(infos, f, d, own, token_weights) for d in range(SIDE)], axis=0)
        scaled.append((hidden[f].astype(F32) * weight).astype(BF16))
    scaled = jnp.concatenate(scaled, axis=0)

    gradient(0)
    err_pass(2)
    reduce_steps(0)
    gradient(1)
    err_pass(3)
    reduce_steps(1)
    for p in range(2, PASSES):
        gradient(p)
        reduce_steps(p)
    for k in range(CUTS):
        value = own_part(0, k)
        for way in range(2):
            pass_on(way, ring_counts[way] - 1, k).wait_recv()
            value = value + ring_in[way, ring_counts[way] - 1, pl.ds(k * cut, cut)]
        grad[k * cut : (k + 1) * cut] = value

    go.finish()
    for step in range(1, SIDE):
        info_x(step).wait_send()
        info_y(step).wait_send()
        share(0, step).wait_send()
        share(1, step).wait_send()
        home(0, step, 0).wait_send()
        for f in range(SIDE):
            home(1, f, step).wait_send()
    for way, count in ((0, ups), (1, downs)):
        for step in range(count):
            gather(way, step).wait_send()
    for p in range(PASSES):
        for half in range(2):
            twin(p, half).wait_send()
            for step in range(1, SIDE):
                err_first(p, half, step).wait_send()
            for a in range(SIDE):
                for hop in range(1, SIDE):
                    f, d = (hop, a) if half == 0 else (a, hop)
                    err_second(p, half, f, d).wait_send()
    for stage in range(4):
        for step in range(1, stage_sizes[stage]):
            tell(stage, step).wait_send()
    for way in range(2):
        for step in range(ring_counts[way]):
            for k in range(CUTS):
                pass_on(way, step, k).wait_send()


def local(nz, tokens, targets, routes, route_logits, slot_order, seq_ids, w_gate, w_up, w_down):
    tok, feat = tokens.shape
    top = routes.shape[1]
    units = w_gate.shape[2]
    scale = float(tok * lax.axis_size("dp") * lax.axis_size("expert") // 8)
    width = feat // 2

    routes_t, logits_t, order_t = routes.T, route_logits.T, slot_order.T
    slots = lax.broadcasted_iota(jnp.int32, (1, top, 1), 1)
    picked = jnp.sum(jnp.where(order_t[:, None, :] == slots, logits_t[None, :, :], 0.0), axis=1)
    raised = jnp.exp(picked)
    gates = raised / jnp.sum(raised, axis=0, keepdims=True)
    hot = routes_t[None, :, :] == lax.broadcasted_iota(jnp.int32, (EXPERTS, 1, 1), 0)
    named = jnp.sum(jnp.where(hot, 1.0, 0.0), axis=1)
    gate_of = jnp.sum(jnp.where(hot, gates[None], 0.0), axis=1)
    earlier = lax.broadcasted_iota(jnp.int32, (tok, tok), 0) < lax.broadcasted_iota(jnp.int32, (tok, tok), 1)
    ranks = jnp.dot(named.astype(BF16), earlier.astype(BF16), preferred_element_type=F32)
    ranks = jnp.where(named > 0.5, ranks, -1.0)
    seq_rows = jnp.broadcast_to(seq_ids.astype(F32)[None, :], (ROWS_INFO - 2 * EXPERTS, tok))
    info = jnp.concatenate([ranks, gate_of, seq_rows], axis=0)

    vmem = pl.BlockSpec(memory_space=pltpu.VMEM)
    dma = pltpu.SemaphoreType.DMA
    travel = [
        pltpu.VMEM((2, SIDE - 1, tok, width), BF16),
        pltpu.VMEM((2, SIDE, SIDE, CAP, width), BF16),
        pltpu.VMEM((2, SIDE, SIDE, CAP, width), BF16),
    ]
    travel_sems = [
        dma((2, SIDE - 1)), dma((2, SIDE - 1)), dma((2, SIDE, SIDE)), dma((2, SIDE, SIDE)),
    ]
    flops = 2 * EXPERTS * CAP * feat * units
    blocks = feat // LANES
    block = LANES // 2
    per = blocks // (2 * PASSES)
    mixed, grad, losses = pl.pallas_call(
        functools.partial(step_kernel, nz, scale),
        out_shape=(
            jax.ShapeDtypeStruct((tok, feat), BF16),
            jax.ShapeDtypeStruct((block, units), F32),
            jax.ShapeDtypeStruct((8, 2 * NSEQ), F32),
        ),
        in_specs=[vmem] * 6,
        out_specs=[vmem] * 3,
        scratch_shapes=[
            pltpu.VMEM((SIDE, SIDE, ROWS_INFO, tok), F32),
            pltpu.VMEM((SIDE, SIDE * CAP, units), BF16),
            pltpu.VMEM((nz, 2, feat // (2 * nz), units), BF16),
            *travel,
            pltpu.VMEM((2, SIDE, SIDE, CAP, width), BF16),
            pltpu.VMEM((2, SIDE, SIDE, CAP, width), BF16),
            pltpu.VMEM((2, SIDE - 1, tok, width), BF16),
            pltpu.VMEM((2, SIDE - 1, tok, width), BF16),
            pltpu.VMEM((blocks, tok, LANES), BF16),
            pltpu.VMEM((PASSES, 2, SIDE - 1, per, tok, LANES), BF16),
            pltpu.VMEM((PASSES, 2, SIDE, SIDE, CAP, per * LANES), BF16),
            pltpu.VMEM((PASSES, 2, SIDE, SIDE, CAP, per * LANES), BF16),
            pltpu.VMEM((4, 2 * SIDE, 8, 2 * NSEQ), F32),
            pltpu.VMEM((blocks, 2, block, units), F32),
            pltpu.VMEM((blocks, block, units), F32),
            pltpu.VMEM((2, blocks // 2, block, units), F32),
            pltpu.VMEM((2, blocks // 2, block, units), F32),
            dma((2, SIDE - 1)), dma((2, SIDE - 1)),
            *travel_sems,
            dma((2, nz // 2 + 1)), dma((2, nz // 2 + 1)),
            dma((2, SIDE, SIDE)), dma((2, SIDE, SIDE)),
            dma((2, SIDE - 1)), dma((2, SIDE - 1)),
            dma((PASSES, 2, SIDE - 1)), dma((PASSES, 2, SIDE - 1)),
            dma((PASSES, 2, SIDE, SIDE)), dma((PASSES, 2, SIDE, SIDE)),
            dma((4, 2 * SIDE)), dma((4, 2 * SIDE)),
            dma((PASSES, 2)), dma((PASSES, 2)),
            dma((2, blocks // 2, CUTS)), dma((2, blocks // 2, CUTS)),
        ],
        compiler_params=pltpu.CompilerParams(
            collective_id=0, has_side_effects=True, vmem_limit_bytes=60 * 2**20
        ),
        cost_estimate=pl.CostEstimate(flops=4 * flops, bytes_accessed=8 * 2**20, transcendentals=0),
        name="robust_step",
    )(tokens, targets, info, w_gate[0], w_up[0], w_down[:, 0])
    return (mixed, losses[0, :NSEQ], losses[1, :NSEQ], grad[:, None, :])


def solution(mesh):
    return jax.shard_map(
        functools.partial(local, mesh.shape["dp"] // 2),
        mesh=mesh,
        in_specs=(
            P(("dp", "expert"), None),
            P(("dp", "expert"), None),
            P(("dp", "expert"), None),
            P(("dp", "expert"), None),
            P(("dp", "expert"), None),
            P(("dp", "expert")),
            P("expert", None, None),
            P("expert", None, None),
            P("dp", "expert", None),
        ),
        out_specs=(P(("dp", "expert"), None), P(), P(), P("dp", "expert", None)),
        check_vma=False,
    )
```

time: 201 us -> 174 us (0.87)
  Pallas kernels: 192 us -> 166 us
    pallas_call x2 -> x1, Pallas kernels: 192 us -> 166 us  [local(): pl.pallas_call(functools.partial(step_kernel, nz, scale), out_shape=(jax....]
where the time goes in v2:
time: 174 us
  Pallas kernels  166 us (95%)
  local copies, waits for them, and re-layouts  4.78 us (3%)
  other arithmetic  2.75 us (2%)
    pallas_call x1, Pallas kernels, local(): pl.pallas_call(functools.partial(step_kernel, nz, scale), out_shape=(jax....  166 us
    unnamed x2, local copies, waits for them, and re-layouts  3.51 us

profile of v2, /device:TPU:1, one launch (start us, length us, event | category | flops | bytes accessed | tf_op | source)
XLA Modules:
  0.0 173.9 jit_solution(8838360736143607154)
XLA Ops:
  0.6 0.7 select_reduce_fusion.2
  1.4 0.7 select_reduce_fusion.1
  2.1 0.1 convolution_select_fusion
  2.3 0.7 convert_element_type.8
  2.9 0.6 pad_maximum_fusion.info
  3.5 165.6 %robust_step.1 = (bf16[128,2048]{1,0:T(8,128)(2,1)}, f32[64,384]{1,0:T(8,128)}, f32[8,128]{1,0:T(8,128)}) custom-call(bf16[128,2048]{1,0:T(8,128)(2,1)} %tokens.1, bf16[128,2048]{1,0:T(8,128)(2,1)} %targets.1, f32[40,128]{1,0:T(8,128)} %pad_maximum_fusion.info, bf16[2048,384]{1,0:T(8,128)(2,1)} %bitcast.15, bf16[2048,384]{1,0:T(8,128)(2,1)} %bitcast.16, ...), custom_call_target="tpu_custom_call" | custom-call | flops 6442450944 | bytes 8388608 | tf_op jit(solution)/shard_map/robust_step/pallas_call | solution.py:581
  169.1 1.3 slice_bitcast_fusion
  170.4 1.6 copy.14
  172.0 1.9 %copy.16 = bf16[128,2048]{1,0:T(8,128)(2,1)} copy(bf16[128,2048]{1,0:T(8,128)(2,1)} %get-tuple-element.26) | data formatting | bytes 1048576
  (3 shorter events, 0.0 us)

commit v3 on v2

--- a/solution.py
+++ b/solution.py
@@ -14,7 +14,7 @@
 EXPERTS = 16
 ROWS_INFO = 40
 PASSES = 4
-CUTS = 4
+CUTS = 2
 LANES = 128
 F32 = jnp.float32
 BF16 = jnp.bfloat16
@@ -89,6 +89,12 @@
         return remote(
             self.sent.at[half, f, d], self.rows.at[half, f, d], self.s2.at[half, f, d], self.r2.at[half, f, d],
             self.peer(1 - half, hop),
+        )
+
+    def late(self, f):
+        part = pl.ds(1, SIDE - 1)
+        return remote(
+            self.sent.at[0, f, part], self.rows.at[0, f, part], self.s2.at[0, f, 1], self.r2.at[0, f, 1], self.peer(1, f)
         )
 
     def start(self):
@@ -115,20 +121,21 @@
                 self.rows[half, f, d] = value
 
     def arrived(self, f):
-        for d in range(SIDE):
-            if f:
-                self.second(0, f, d).wait_recv()
-            if d:
-                self.second(1, f, d).wait_recv()
+        if f:
+            self.second(0, f, 0).wait_recv()
+            self.late(f).wait_recv()
+        for d in range(1, SIDE):
+            self.second(1, f, d).wait_recv()
 
     def finish(self):
         for half in range(2):
             for step in range(1, SIDE):
                 self.first(half, step).wait_send()
-            for a in range(SIDE):
-                for hop in range(1, SIDE):
-                    f, d = (hop, a) if half == 0 else (a, hop)
-                    self.second(half, f, d).wait_send()
+        for hop in range(1, SIDE):
+            self.second(0, hop, 0).wait_send()
+            self.late(hop).wait_send()
+            for f in range(SIDE):
+                self.second(1, f, hop).wait_send()
 
 
 def dual_search(loss_column):
@@ -175,10 +182,10 @@
     own = x * SIDE + y
     ring = lambda dz: place(*here, dz=dz, nz=nz)
     twin_device = place(*here, other=True)
-    low, high = z % SIDE, z // SIDE
     around = lambda index, step, size: lax.rem(index + step, size)
-    stage_sizes = (SIDE, 2 * SIDE, SIDE, SIDE)
-    stage_index = (x, y * 2 + core, low, high)
+    stage_sizes = (SIDE, 2 * SIDE, nz)
+    stage_index = (x, y * 2 + core, z)
+    stages = len(stage_sizes)
 
     def stage_device(stage, step):
         if stage == 0:
@@ -186,12 +193,9 @@
         if stage == 1:
             to = around(y * 2 + core, step, 2 * SIDE)
             return {"dp": z * 2 + to % 2, "expert": x * SIDE + to // 2}
-        if stage == 2:
-            return {"dp": (high * SIDE + around(low, step, SIDE)) * 2 + core, "expert": own}
-        return {"dp": (around(high, step, SIDE) * SIDE + low) * 2 + core, "expert": own}
-
-    peers = [stage_device(stage, step) for stage in range(4) for step in range(1, stage_sizes[stage])]
-    peers += [ring(1), ring(-1)]
+        return {"dp": around(z, step, nz) * 2 + core, "expert": own}
+
+    peers = [stage_device(stage, step) for stage in range(stages) for step in range(1, stage_sizes[stage])]
     meet(peers)
 
     infos[0, 0] = info[...]
@@ -200,10 +204,17 @@
         return remote(info, infos.at[0, step], i_s.at[0, step - 1], i_r.at[0, step - 1], place(*here, dx=step))
 
     def info_y(step):
-        return remote(infos.at[0], infos.at[step], i_s.at[1, step - 1], i_r.at[1, step - 1], place(*here, dy=step))
+        return remote(info, infos.at[step, 0], i_s.at[1, step - 1], i_r.at[1, step - 1], place(*here, dy=step))
+
+    def info_relay(step):
+        part = pl.ds(1, SIDE - 1)
+        return remote(
+            infos.at[0, part], infos.at[step, part], i_s.at[2, step - 1], i_r.at[2, step - 1], place(*here, dy=step)
+        )
 
     for step in range(1, SIDE):
         info_x(step).start()
+        info_y(step).start()
     go = Dispatch(tokens, wide, sent, rows, s1, r1, s2, r2, here)
     go.start()
 
@@ -226,12 +237,12 @@
 
     gather_step(0)
     go.forward(infos, 1, 0)
-    go.forward(infos, 0, 0, send=False)
+    go.forward(infos, 0, 0)
     gather_step(1)
     for step in range(1, SIDE):
         info_x(step).wait_recv()
     for step in range(1, SIDE):
-        info_y(step).start()
+        info_relay(step).start()
     gather_step(2)
     tick = 3
     for step in (1, 3, 2):
@@ -241,8 +252,7 @@
     for step in range(1, SIDE):
         info_y(step).wait_recv()
     for f in (1, 3, 2):
-        for d in range(SIDE):
-            go.second(0, f, d).start()
+        go.late(f).start()
         go.forward(infos, 1, f)
         gather_step(tick)
         tick += 1
@@ -252,6 +262,8 @@
         remote(down.at[:, side], down.at[:, side], w_s.at[0, ups], w_r.at[0, ups], twin_device) for side in (core, 1 - core)
     ]
     twin_down[0].start()
+    for step in range(1, SIDE):
+        info_relay(step).wait_recv()
 
     def home(half, f, d):
         if half == 0:
@@ -359,7 +371,7 @@
         value = seen[stage, 0]
         for index in range(1, stage_sizes[stage]):
             value = value + seen[stage, index]
-        if stage < 3:
+        if stage + 1 < stages:
             stage_start(stage + 1, value)
         return value
 
@@ -377,10 +389,14 @@
             e1s.at[p, half, step - 1], e1r.at[p, half, step - 1], device,
         )
 
-    def err_second(p, half, f, d):
-        device = place(*here, dy=f) if half == 0 else place(*here, dx=d)
-        return remote(
-            err_sent.at[p, half, f, d], err_rows.at[p, half, f, d], e2s.at[p, half, f, d], e2r.at[p, half, f, d], device
+    def err_second(p, half, hop, late):
+        device = place(*here, dy=hop) if half == 0 else place(*here, dx=hop)
+        part = pl.ds(0, SIDE)
+        if p == 0:
+            part = pl.ds(1, SIDE - 1) if late else pl.ds(0, 1)
+        return remote(
+            err_sent.at[p, half, hop, part], err_rows.at[p, half, hop, part],
+            e2s.at[p, half, hop, late], e2r.at[p, half, hop, late], device,
         )
 
     def err_start(p):
@@ -396,25 +412,19 @@
             block = jnp.concatenate([err[span(half, p) + i] for i in range(per)], axis=1)
         picked = jnp.dot(selection(infos, half, step, x, y), block, preferred_element_type=F32)
         for hop in (2, 1, 3, 0):
-            f, d = (hop, step) if half == 0 else (step, hop)
             value = picked[hop * CAP : (hop + 1) * CAP].astype(BF16)
             if hop:
-                err_sent[p, half, f, d] = value
-                err_second(p, half, f, d).start()
+                err_sent[p, half, hop, step] = value
+                if step == 2 or (p == 0 and step == 0):
+                    err_second(p, half, hop, int(step == 2)).start()
             else:
-                err_rows[p, half, f, d] = value
-
-    def err_pass(p):
-        for step in (0, 1, 3, 2):
-            for half in range(2):
-                err_forward(p, half, step)
+                err_rows[p, half, 0, step] = value
 
     def err_arrived(p):
         for half in range(2):
-            for a in range(SIDE):
-                for hop in range(1, SIDE):
-                    f, d = (hop, a) if half == 0 else (a, hop)
-                    err_second(p, half, f, d).wait_recv()
+            for hop in range(1, SIDE):
+                for late in range(1 if p else 0, 2):
+                    err_second(p, half, hop, late).wait_recv()
 
     block_rows = LANES // 2
 
@@ -425,8 +435,14 @@
     def gradient(p):
         err_arrived(p)
         for half in range(2):
+            if half == 0:
+                block = err_rows[p, 0].reshape(SIDE * SIDE * CAP, per * LANES)
+            else:
+                block = jnp.concatenate(
+                    [err_rows[p, 1, :, f].reshape(SIDE * CAP, per * LANES) for f in range(SIDE)], axis=0
+                )
             value = lax.dot_general(
-                err_rows[p, half].reshape(SIDE * SIDE * CAP, per * LANES), scaled,
+                block, scaled,
                 (((0,), (0,)), ((), ())), preferred_element_type=F32,
             )
             grads[span(half, p) : span(half, p) + per] = value.reshape(per, 2, block_rows, -1)
@@ -461,20 +477,22 @@
                         ring_out[way, step, pl.ds(k * cut, cut)] = value
                         pass_on(way, step, k).start()
 
+    def err_both(p, *steps):
+        for step in steps:
+            for half in range(2):
+                err_forward(p, half, step)
+
     err_start(0)
-    for half in range(2):
-        err_forward(0, half, 0)
+    err_both(0, 0)
     err_start(1)
+    err_both(0, 1)
     stage_end(0)
-    for stage, step in ((1, 1), (2, 3)):
-        for half in range(2):
-            err_forward(0, half, step)
-        stage_end(stage)
-    for half in range(2):
-        err_forward(0, half, 2)
+    err_both(0, 3, 2)
+    stage_end(1)
+    err_both(1, 0)
     err_start(2)
-    err_pass(1)
-    sums = stage_end(3)[0:1]
+    err_both(1, 1, 3, 2)
+    sums = stage_end(2)[0:1]
     err_start(3)
     lengths = pltpu.roll(sums, NSEQ, 1)
     loss_row = sums / (lengths * float(feat))
@@ -498,10 +516,10 @@
     scaled = jnp.concatenate(scaled, axis=0)
 
     gradient(0)
-    err_pass(2)
+    err_both(2, 0, 1, 3, 2)
     reduce_steps(0)
     gradient(1)
-    err_pass(3)
+    err_both(3, 0, 1, 3, 2)
     reduce_steps(1)
     for p in range(2, PASSES):
         gradient(p)
@@ -517,6 +535,7 @@
     for step in range(1, SIDE):
         info_x(step).wait_send()
         info_y(step).wait_send()
+        info_relay(step).wait_send()
         share(0, step).wait_send()
         share(1, step).wait_send()
         home(0, step, 0).wait_send()
@@ -530,11 +549,10 @@
             twin(p, half).wait_send()
             for step in range(1, SIDE):
                 err_first(p, half, step).wait_send()
-            for a in range(SIDE):
-                for hop in range(1, SIDE):
-                    f, d = (hop, a) if half == 0 else (a, hop)
-                    err_second(p, half, f, d).wait_send()
-    for stage in range(4):
+            for hop in range(1, SIDE):
+                for late in range(1 if p else 0, 2):
+                    err_second(p, half, hop, late).wait_send()
+    for stage in range(stages):
         for step in range(1, stage_sizes[stage]):
             tell(stage, step).wait_send()
     for way in range(2):
@@ -600,19 +618,19 @@
             pltpu.VMEM((PASSES, 2, SIDE - 1, per, tok, LANES), BF16),
             pltpu.VMEM((PASSES, 2, SIDE, SIDE, CAP, per * LANES), BF16),
             pltpu.VMEM((PASSES, 2, SIDE, SIDE, CAP, per * LANES), BF16),
-            pltpu.VMEM((4, 2 * SIDE, 8, 2 * NSEQ), F32),
+            pltpu.VMEM((3, max(2 * SIDE, nz), 8, 2 * NSEQ), F32),
             pltpu.VMEM((blocks, 2, block, units), F32),
             pltpu.VMEM((blocks, block, units), F32),
             pltpu.VMEM((2, blocks // 2, block, units), F32),
             pltpu.VMEM((2, blocks // 2, block, units), F32),
-            dma((2, SIDE - 1)), dma((2, SIDE - 1)),
+            dma((3, SIDE - 1)), dma((3, SIDE - 1)),
             *travel_sems,
             dma((2, nz // 2 + 1)), dma((2, nz // 2 + 1)),
             dma((2, SIDE, SIDE)), dma((2, SIDE, SIDE)),
             dma((2, SIDE - 1)), dma((2, SIDE - 1)),
             dma((PASSES, 2, SIDE - 1)), dma((PASSES, 2, SIDE - 1)),
-            dma((PASSES, 2, SIDE, SIDE)), dma((PASSES, 2, SIDE, SIDE)),
-            dma((4, 2 * SIDE)), dma((4, 2 * SIDE)),
+            dma((PASSES, 2, SIDE, 2)), dma((PASSES, 2, SIDE, 2)),
+            dma((3, max(2 * SIDE, nz))), dma((3, max(2 * SIDE, nz))),
             dma((PASSES, 2)), dma((PASSES, 2)),
             dma((2, blocks // 2, CUTS)), dma((2, blocks // 2, CUTS)),
         ],

time: 174 us -> 168 us (0.966)
  Pallas kernels: 166 us -> 160 us
    pallas_call x1, Pallas kernels: 166 us -> 160 us  [local(): pl.pallas_call(functools.partial(step_kernel, nz, scale), out_shape=(jax....]
where the time goes in v3:
time: 168 us
  Pallas kernels  160 us (95%)
  local copies, waits for them, and re-layouts  4.78 us (3%)
  other arithmetic  2.75 us (2%)
    pallas_call x1, Pallas kernels, local(): pl.pallas_call(functools.partial(step_kernel, nz, scale), out_shape=(jax....  160 us
    unnamed x2, local copies, waits for them, and re-layouts  3.51 us

profile of v3, /device:TPU:1, one launch (start us, length us, event | category | flops | bytes accessed | tf_op | source)
XLA Modules:
  0.0 167.9 jit_solution(10128878360865670750)
XLA Ops:
  0.6 0.7 select_reduce_fusion.2
  1.4 0.7 select_reduce_fusion.1
  2.1 0.1 convolution_select_fusion
  2.3 0.7 convert_element_type.8
  2.9 0.6 pad_maximum_fusion.info
  3.5 159.6 %robust_step.1 = (bf16[128,2048]{1,0:T(8,128)(2,1)}, f32[64,384]{1,0:T(8,128)}, f32[8,128]{1,0:T(8,128)}) custom-call(bf16[128,2048]{1,0:T(8,128)(2,1)} %tokens.1, bf16[128,2048]{1,0:T(8,128)(2,1)} %targets.1, f32[40,128]{1,0:T(8,128)} %pad_maximum_fusion.info, bf16[2048,384]{1,0:T(8,128)(2,1)} %bitcast.15, bf16[2048,384]{1,0:T(8,128)(2,1)} %bitcast.16, ...), custom_call_target="tpu_custom_call" | custom-call | flops 6442450944 | bytes 8388608 | tf_op jit(solution)/shard_map/robust_step/pallas_call | solution.py:599
  163.1 1.3 slice_bitcast_fusion
  164.4 1.6 copy.14
  166.0 1.9 %copy.16 = bf16[128,2048]{1,0:T(8,128)(2,1)} copy(bf16[128,2048]{1,0:T(8,128)(2,1)} %get-tuple-element.26) | data formatting | bytes 1048576
  (3 shorter events, 0.0 us)

commit v4 on v3

--- a/solution.py
+++ b/solution.py
@@ -39,11 +39,31 @@
     )
 
 
-def meet(devices):
+def meet(devices, meanwhile):
     barrier = pltpu.get_barrier_semaphore()
     for device in devices:
         pl.semaphore_signal(barrier, inc=1, device_id=device, device_id_type=MESH)
+    meanwhile()
     pl.semaphore_wait(barrier, len(devices))
+
+
+def routing(routes, logits, order, seq_ids, info):
+    top, tok = routes.shape
+    slots = lax.broadcasted_iota(jnp.int32, (top, tok), 0)
+    experts = lax.broadcasted_iota(jnp.int32, (EXPERTS, tok), 0)
+    named = jnp.zeros((EXPERTS, tok), F32)
+    gates = jnp.zeros((EXPERTS, tok), F32)
+    for k in range(top):
+        score = jnp.sum(jnp.where(order[k : k + 1, :] == slots, logits[...], 0.0), axis=0, keepdims=True)
+        hot = routes[k : k + 1, :] == experts
+        named = jnp.where(hot, 1.0, named)
+        gates = jnp.where(hot, jnp.exp(score), gates)
+    gates = gates / jnp.sum(gates, axis=0, keepdims=True)
+    earlier = lax.broadcasted_iota(jnp.int32, (tok, tok), 0) < lax.broadcasted_iota(jnp.int32, (tok, tok), 1)
+    ranks = jnp.dot(named.astype(BF16), jnp.where(earlier, 1.0, 0.0).astype(BF16), preferred_element_type=F32)
+    info[0:EXPERTS, :] = jnp.where(named > 0.5, ranks, -1.0)
+    info[EXPERTS : 2 * EXPERTS, :] = gates
+    info[2 * EXPERTS :, :] = jnp.broadcast_to(seq_ids[...].astype(F32), (ROWS_INFO - 2 * EXPERTS, tok))
 
 
 def hot_rows(rank_row):
@@ -168,9 +188,9 @@
 
 
 def step_kernel(
-    nz, scale, tokens, targets, info, w_gate, w_up, w_down,
+    nz, scale, tokens, targets, routes, route_logits, slot_order, seq_ids, w_gate, w_up, w_down,
     mixed, grad, losses,
-    infos, hidden, down, wide, sent, rows, outs, back, part_out, part_in,
+    info, infos, hidden, down, wide, sent, rows, outs, back, part_out, part_in,
     err, err_wide, err_sent, err_rows, seen, grads, twin_in, ring_out, ring_in,
     i_s, i_r, s1, r1, s2, r2, w_s, w_r, b_s, b_r, p_s, p_r,
     e1s, e1r, e2s, e2r, a_s, a_r, t_s, t_r, g_s, g_r,
@@ -196,7 +216,7 @@
         return {"dp": around(z, step, nz) * 2 + core, "expert": own}
 
     peers = [stage_device(stage, step) for stage in range(stages) for step in range(1, stage_sizes[stage])]
-    meet(peers)
+    meet(peers, lambda: routing(routes, route_logits, slot_order, seq_ids, info))
 
     infos[0, 0] = info[...]
 
@@ -563,24 +583,9 @@
 
 def local(nz, tokens, targets, routes, route_logits, slot_order, seq_ids, w_gate, w_up, w_down):
     tok, feat = tokens.shape
-    top = routes.shape[1]
     units = w_gate.shape[2]
     scale = float(tok * lax.axis_size("dp") * lax.axis_size("expert") // 8)
     width = feat // 2
-
-    routes_t, logits_t, order_t = routes.T, route_logits.T, slot_order.T
-    slots = lax.broadcasted_iota(jnp.int32, (1, top, 1), 1)
-    picked = jnp.sum(jnp.where(order_t[:, None, :] == slots, logits_t[None, :, :], 0.0), axis=1)
-    raised = jnp.exp(picked)
-    gates = raised / jnp.sum(raised, axis=0, keepdims=True)
-    hot = routes_t[None, :, :] == lax.broadcasted_iota(jnp.int32, (EXPERTS, 1, 1), 0)
-    named = jnp.sum(jnp.where(hot, 1.0, 0.0), axis=1)
-    gate_of = jnp.sum(jnp.where(hot, gates[None], 0.0), axis=1)
-    earlier = lax.broadcasted_iota(jnp.int32, (tok, tok), 0) < lax.broadcasted_iota(jnp.int32, (tok, tok), 1)
-    ranks = jnp.dot(named.astype(BF16), earlier.astype(BF16), preferred_element_type=F32)
-    ranks = jnp.where(named > 0.5, ranks, -1.0)
-    seq_rows = jnp.broadcast_to(seq_ids.astype(F32)[None, :], (ROWS_INFO - 2 * EXPERTS, tok))
-    info = jnp.concatenate([ranks, gate_of, seq_rows], axis=0)
 
     vmem = pl.BlockSpec(memory_space=pltpu.VMEM)
     dma = pltpu.SemaphoreType.DMA
@@ -603,9 +608,10 @@
             jax.ShapeDtypeStruct((block, units), F32),
             jax.ShapeDtypeStruct((8, 2 * NSEQ), F32),
         ),
-        in_specs=[vmem] * 6,
+        in_specs=[vmem] * 9,
         out_specs=[vmem] * 3,
         scratch_shapes=[
+            pltpu.VMEM((ROWS_INFO, tok), F32),
             pltpu.VMEM((SIDE, SIDE, ROWS_INFO, tok), F32),
             pltpu.VMEM((SIDE, SIDE * CAP, units), BF16),
             pltpu.VMEM((nz, 2, feat // (2 * nz), units), BF16),
@@ -639,7 +645,7 @@
         ),
         cost_estimate=pl.CostEstimate(flops=4 * flops, bytes_accessed=8 * 2**20, transcendentals=0),
         name="robust_step",
-    )(tokens, targets, info, w_gate[0], w_up[0], w_down[:, 0])
+    )(tokens, targets, routes.T, route_logits.T, slot_order.T, seq_ids[None, :], w_gate[0], w_up[0], w_down[:, 0])
     return (mixed, losses[0, :NSEQ], losses[1, :NSEQ], grad[:, None, :])
 
 

time: 168 us -> 165 us (0.982)
  other arithmetic: 2.75 us -> 0 us
where the time goes in v4:
time: 165 us
  Pallas kernels  159 us (96%)
  local copies, waits for them, and re-layouts  4.77 us (3%)
    pallas_call x1, Pallas kernels, local(): pl.pallas_call(functools.partial(step_kernel, nz, scale), out_shape=(jax....  159 us
    unnamed x2, local copies, waits for them, and re-layouts  3.51 us

profile of v4, /device:TPU:1, one launch (start us, length us, event | category | flops | bytes accessed | tf_op | source)
XLA Modules:
  0.0 164.8 jit_solution(1871997170966459238)
XLA Ops:
  0.6 159.4 %robust_step.1 = (bf16[128,2048]{1,0:T(8,128)(2,1)}, f32[64,384]{1,0:T(8,128)}, f32[8,128]{1,0:T(8,128)}) custom-call(bf16[128,2048]{1,0:T(8,128)(2,1)} %tokens.1, bf16[128,2048]{1,0:T(8,128)(2,1)} %targets.1, s32[8,128]{1,0:T(8,128)} %bitcast.16, f32[8,128]{1,0:T(8,128)} %bitcast.17, s32[8,128]{1,0:T(8,128)} %bitcast.18, s32[1,128]{1,0:T(1,128)} %bitcast.19, ...), custom_call_target="tpu_custom_call" | custom-call | flops 6442450944 | bytes 8388608 | tf_op jit(solution)/shard_map/robust_step/pallas_call | solution.py:604
  160.0 1.3 slice_bitcast_fusion
  161.3 1.6 copy.13
  162.9 1.9 %copy.15 = bf16[128,2048]{1,0:T(8,128)(2,1)} copy(bf16[128,2048]{1,0:T(8,128)(2,1)} %get-tuple-element.20) | data formatting | bytes 1048576
